TPU v7x, 512 devices: a whole 4x8x8 slice. The times are simulated.
512 devices in a mesh: seq: 32 (over z, x_hi, core), tensor: 16 (over y, x_lo).
Axes of the slice: x: 4 (x_hi: 2, x_lo: 2; x = x_hi * 2 + x_lo), y: 8, z: 8, core: 2. Of those that a mesh axis runs over, the one named last changes fastest.
Arguments:
- query: bfloat16 [8192, 4096], P('seq', 'tensor'), may hold values from -6 to 6
- key_branch: bfloat16 [8192, 4096], P('seq', 'tensor'), may hold values from -6 to 6
- value: bfloat16 [8192, 4096], P('seq', 'tensor'), may hold values from -6 to 6
- filters: float32 [256, 8192], P('tensor', 'seq'), may hold values from -4 to 4
- skip: float32 [4096], P('tensor'), may hold values from -4 to 4
- weight: bfloat16 [4096, 8192], P('tensor'), may hold values from -0.09375 to 0.09375
Outputs:
- layer_out: bfloat16 [8192, 8192], P(('seq', 'tensor'))
All inputs are finite; a program needn't handle non-finite values.
Results may differ from a plain program's by a relative error of at most 0.029.
Values may be sent and summed in bfloat16 or wider, within the bound.
A program may use at most 64 MiB of HBM per device.

v0:
```python
import math

import jax
import jax.numpy as jnp
from jax import lax
from jax.sharding import PartitionSpec as P

GROUP = 16


TWO_PI = 2.0 * math.pi


def from_partner(value, axis, apart):
    mask = 2**apart
    pairs = [(source, source ^ mask) for source in range(lax.axis_size(axis))]
    return lax.ppermute(value, axis, pairs)


def rotate(pair, angle):
    cosine = jnp.cos(angle)
    sine = jnp.sin(angle)
    return jnp.stack([pair[0] * cosine - pair[1] * sine, pair[0] * sine + pair[1] * cosine])


def complex_product(left, right):
    return jnp.stack(
        [left[0] * right[0] - left[1] * right[1], left[0] * right[1] + left[1] * right[0]]
    )


def transform_last(state, sign):
    extent = state.shape[-1]
    counter = jnp.arange(extent, dtype=jnp.int32)
    angle = (counter[:, None] * counter[None, :] % extent).astype(jnp.float32) * (
        sign * TWO_PI / extent
    )
    cosine = jnp.cos(angle)
    sine = jnp.sin(angle)
    highest = lax.Precision.HIGHEST
    real_part = jnp.matmul(state[0], cosine, precision=highest) - jnp.matmul(
        state[1], sine, precision=highest
    )
    imag_part = jnp.matmul(state[0], sine, precision=highest) + jnp.matmul(
        state[1], cosine, precision=highest
    )
    return jnp.stack([real_part, imag_part])


def twist(state, residue, extent, length, sign):
    counter = jnp.arange(extent, dtype=jnp.int32)
    angle = (counter * residue % length).astype(jnp.float32) * (sign * TWO_PI / length)
    return rotate(state, angle)


def first_section(signal, positions, padded):
    odd_part = rotate(signal, positions.astype(jnp.float32) * (-TWO_PI / padded))
    return jnp.stack([signal, odd_part], axis=1)


def last_section(state, positions, padded):
    odd_part = rotate(state[:, 1], positions.astype(jnp.float32) * (TWO_PI / padded))
    return (state[:, 0] + odd_part) / padded


def reversed_index(index, levels):
    total = jnp.zeros((), jnp.int32)
    for digit in range(levels):
        total = total + index // 2**digit % 2 * 2 ** (levels - 1 - digit)
    return total


def butterfly_cross(state, sign, index, levels):
    if sign > 0:
        order = range(levels)
    else:
        order = range(levels - 1, -1, -1)
    for digit in order:
        span = 2**digit
        partner = from_partner(state.astype(jnp.bfloat16), "seq", digit).astype(state.dtype)
        upper = index // span % 2 == 1
        angle = (index % span).astype(jnp.float32) * (sign * math.pi / span)
        if sign < 0:
            lower_value = state + partner
            upper_value = rotate(partner - state, angle)
        else:
            lower_value = state + rotate(partner, angle)
            upper_value = partner - rotate(state, angle)
        state = jnp.where(upper, upper_value, lower_value)
    return state


def slab_path(packed, filters, index, levels, crossing, residue):
    groups, extent = filters.shape
    length = extent * 2**levels
    padded = 2 * length
    positions = index * extent + jnp.arange(extent, dtype=jnp.int32)
    taps = jnp.stack([filters, jnp.zeros_like(filters)])
    state = first_section(jnp.concatenate([packed, taps], axis=1), positions, padded)
    state = crossing(state, -1.0, index, levels)
    state = transform_last(twist(state, residue, extent, length, -1.0), -1.0)
    signal_columns = packed.shape[1]
    spectrum = state[:, :, :signal_columns].reshape(2, 2, groups, signal_columns // groups, extent)
    filter_spectrum = state[:, :, signal_columns:][:, :, :, None, :]
    product = complex_product(spectrum, filter_spectrum).reshape(2, 2, signal_columns, extent)
    back = twist(transform_last(product, 1.0), residue, extent, length, 1.0)
    back = crossing(back, 1.0, index, levels)
    return last_section(back, positions, padded)


def body(query, key_branch, value, filters, skip, weight):
    extent, width = query.shape
    groups = filters.shape[0]
    index = lax.axis_index("seq")
    levels = lax.axis_size("seq").bit_length() - 1
    mixed = key_branch.astype(jnp.float32) * value.astype(jnp.float32)
    half = GROUP // 2
    shaped = mixed.T.reshape(groups, GROUP, extent)
    packed = jnp.stack(
        [
            shaped[:, :half].reshape(groups * half, extent),
            shaped[:, half:].reshape(groups * half, extent),
        ]
    )
    result = slab_path(
        packed, filters, index, levels, butterfly_cross, reversed_index(index, levels)
    )
    unpacked = jnp.concatenate(
        [result[0].reshape(groups, half, extent), result[1].reshape(groups, half, extent)], axis=1
    )
    response = unpacked.reshape(width, extent).T
    gated = (query.astype(jnp.float32) * (response + skip[None, :] * mixed)).astype(jnp.bfloat16)
    return lax.psum_scatter(
        jnp.dot(gated, weight, preferred_element_type=jnp.float32).astype(jnp.bfloat16),
        "tensor",
        scatter_dimension=0,
        tiled=True,
    )


def solution(mesh):
    return jax.shard_map(
        body,
        mesh=mesh,
        in_specs=(
            P("seq", "tensor"),
            P("seq", "tensor"),
            P("seq", "tensor"),
            P("tensor", "seq"),
            P("tensor"),
            P("tensor", None),
        ),
        out_specs=P(("seq", "tensor"), None),
        check_vma=False,
    )
```

profile of v0, /device:TPU:6, one launch (start us, length us, event | category | flops | bytes accessed | tf_op | source)
XLA Modules:
  0.0 260.4 jit_solution(1349544166068296521)
XLA Ops:
  9.6 10.9 %collective-permute-start = (bf16[2,2,144,256]{3,2,1,0:T(8,128)(2,1)S(1)}, bf16[2,2,144,256]{3,2,1,0:T(8,128)(2,1)S(1)}, u32[]{:S(2)}, u32[]{:S(2)}) collective-permute-start(bf16[2,2,144,256]{3,2,1,0:T(8,128)(2,1)S(1)} %fusion.13), channel_id=1, source_target_pairs={{0,256},{16,272},{32,288},{48,304},{64,320},{80,336},{96,352},{112... | collective-permute-start | bytes 884744 | tf_op jit(solution)/shard_map/ppermute | solution.py:17
  20.7 6.9 %collective-permute-done = bf16[2,2,144,256]{3,2,1,0:T(8,128)(2,1)S(1)} collective-permute-done((bf16[2,2,144,256]{3,2,1,0:T(8,128)(2,1)S(1)}, bf16[2,2,144,256]{3,2,1,0:T(8,128)(2,1)S(1)}, u32[]{:S(2)}, u32[]{:S(2)}) %collective-permute-start) | collective-permute-done | bytes 294944 | tf_op jit(solution)/shard_map/ppermute | solution.py:17
  27.9 10.5 %collective-permute-start.1 = (bf16[2,2,144,256]{3,2,1,0:T(8,128)(2,1)S(1)}, bf16[2,2,144,256]{3,2,1,0:T(8,128)(2,1)S(1)}, u32[]{:S(2)}, u32[]{:S(2)}) collective-permute-start(bf16[2,2,144,256]{3,2,1,0:T(8,128)(2,1)S(1)} %get-tuple-element.22), channel_id=1, source_target_pairs={{0,128},{16,144},{32,160},{48,176},{64,192},{80,208},{96,224},{112... | collective-permute-start | bytes 884744 | tf_op jit(solution)/shard_map/ppermute | solution.py:17
  38.6 13.2 %collective-permute-done.1 = bf16[2,2,144,256]{3,2,1,0:T(8,128)(2,1)S(1)} collective-permute-done((bf16[2,2,144,256]{3,2,1,0:T(8,128)(2,1)S(1)}, bf16[2,2,144,256]{3,2,1,0:T(8,128)(2,1)S(1)}, u32[]{:S(2)}, u32[]{:S(2)}) %collective-permute-start.1) | collective-permute-done | bytes 294944 | tf_op jit(solution)/shard_map/ppermute | solution.py:17
  52.1 1.9 collective-permute-start.2
  54.2 8.3 %collective-permute-done.2 = bf16[2,2,144,256]{3,2,1,0:T(8,128)(2,1)S(1)} collective-permute-done((bf16[2,2,144,256]{3,2,1,0:T(8,128)(2,1)S(1)}, bf16[2,2,144,256]{3,2,1,0:T(8,128)(2,1)S(1)}, u32[]{:S(2)}, u32[]{:S(2)}) %collective-permute-start.2) | collective-permute-done | bytes 294944 | tf_op jit(solution)/shard_map/ppermute | solution.py:17
  62.7 3.3 %collective-permute-start.3 = (bf16[2,2,144,256]{3,2,1,0:T(8,128)(2,1)S(1)}, bf16[2,2,144,256]{3,2,1,0:T(8,128)(2,1)S(1)}, u32[]{:S(2)}, u32[]{:S(2)}) collective-permute-start(bf16[2,2,144,256]{3,2,1,0:T(8,128)(2,1)S(1)} %get-tuple-element.18), channel_id=1, source_target_pairs={{0,32},{16,48},{32,0},{48,16},{64,96},{80,112},{96,64},{112,80},{1... | collective-permute-start | bytes 884744 | tf_op jit(solution)/shard_map/ppermute | solution.py:17
  66.3 7.5 %collective-permute-done.3 = bf16[2,2,144,256]{3,2,1,0:T(8,128)(2,1)S(1)} collective-permute-done((bf16[2,2,144,256]{3,2,1,0:T(8,128)(2,1)S(1)}, bf16[2,2,144,256]{3,2,1,0:T(8,128)(2,1)S(1)}, u32[]{:S(2)}, u32[]{:S(2)}) %collective-permute-start.3) | collective-permute-done | bytes 294944 | tf_op jit(solution)/shard_map/ppermute | solution.py:17
  74.0 2.1 collective-permute-start.4
  77.7 1.4 fusion.28
  79.1 1.4 fusion.32
  81.9 1.4 fusion.1
  87.4 1.4 subtract_bitcast_fusion
  88.9 2.0 collective-permute-start.5
  92.6 3.5 %collective-permute-start.6 = (bf16[2,2,128,256]{3,2,1,0:T(8,128)(2,1)S(1)}, bf16[2,2,128,256]{3,2,1,0:T(8,128)(2,1)S(1)}, u32[]{:S(2)}, u32[]{:S(2)}) collective-permute-start(bf16[2,2,128,256]{3,2,1,0:T(8,128)(2,1)S(1)} %get-tuple-element.11), channel_id=1, source_target_pairs={{0,32},{16,48},{32,0},{48,16},{64,96},{80,112},{96,64},{112,80},{1... | collective-permute-start | bytes 786440 | tf_op jit(solution)/shard_map/ppermute | solution.py:17
  96.3 8.0 %collective-permute-done.6 = bf16[2,2,128,256]{3,2,1,0:T(8,128)(2,1)S(1)} collective-permute-done((bf16[2,2,128,256]{3,2,1,0:T(8,128)(2,1)S(1)}, bf16[2,2,128,256]{3,2,1,0:T(8,128)(2,1)S(1)}, u32[]{:S(2)}, u32[]{:S(2)}) %collective-permute-start.6) | collective-permute-done | bytes 262176 | tf_op jit(solution)/shard_map/ppermute | solution.py:17
  104.6 2.5 collective-permute-start.7
  107.3 6.7 %collective-permute-done.7 = bf16[2,2,128,256]{3,2,1,0:T(8,128)(2,1)S(1)} collective-permute-done((bf16[2,2,128,256]{3,2,1,0:T(8,128)(2,1)S(1)}, bf16[2,2,128,256]{3,2,1,0:T(8,128)(2,1)S(1)}, u32[]{:S(2)}, u32[]{:S(2)}) %collective-permute-start.7) | collective-permute-done | bytes 262176 | tf_op jit(solution)/shard_map/ppermute | solution.py:17
  114.2 1.9 collective-permute-start.8
  116.4 12.9 %collective-permute-done.8 = bf16[2,2,128,256]{3,2,1,0:T(8,128)(2,1)S(1)} collective-permute-done((bf16[2,2,128,256]{3,2,1,0:T(8,128)(2,1)S(1)}, bf16[2,2,128,256]{3,2,1,0:T(8,128)(2,1)S(1)}, u32[]{:S(2)}, u32[]{:S(2)}) %collective-permute-start.8) | collective-permute-done | bytes 262176 | tf_op jit(solution)/shard_map/ppermute | solution.py:17
  129.5 7.9 %collective-permute-start.9 = (bf16[2,2,128,256]{3,2,1,0:T(8,128)(2,1)S(1)}, bf16[2,2,128,256]{3,2,1,0:T(8,128)(2,1)S(1)}, u32[]{:S(2)}, u32[]{:S(2)}) collective-permute-start(bf16[2,2,128,256]{3,2,1,0:T(8,128)(2,1)S(1)} %get-tuple-element.5), channel_id=1, source_target_pairs={{0,256},{16,272},{32,288},{48,304},{64,320},{80,336},{96,352},{112... | collective-permute-start | bytes 786440 | tf_op jit(solution)/shard_map/ppermute | solution.py:17
  137.8 11.6 %collective-permute-done.9 = bf16[2,2,128,256]{3,2,1,0:T(8,128)(2,1)S(1)} collective-permute-done((bf16[2,2,128,256]{3,2,1,0:T(8,128)(2,1)S(1)}, bf16[2,2,128,256]{3,2,1,0:T(8,128)(2,1)S(1)}, u32[]{:S(2)}, u32[]{:S(2)}) %collective-permute-start.9) | collective-permute-done | bytes 262176 | tf_op jit(solution)/shard_map/ppermute | solution.py:17
  149.9 3.2 %convolution_convert_fusion = bf16[256,8192]{1,0:T(8,128)(2,1)} fusion(bf16[256,256]{0,1:T(8,128)(2,1)S(1)} %fusion.21, bf16[256,8192]{1,0:T(8,128)(2,1)S(1)} %copy-done), kind=kOutput, calls=%fused_computation | convolution fusion | flops 1075838976 | bytes 8519680 | tf_op jit(solution)/shard_map/dot_general | solution.py:134
  153.2 100.3 %reduce-scatter.2.cloned.1.call-done = bf16[16,8192]{1,0:T(8,128)(2,1)} async-done(((bf16[256,8192]{1,0:T(8,128)(2,1)}), bf16[16,8192]{1,0:T(8,128)(2,1)}) %reduce-scatter.2.cloned.1.call-update) | async-done | bytes 262160 | tf_op jit(solution)/shard_map/reduce_scatter | solution.py:133
  (70 shorter events, 14.0 us)
Async XLA Ops:
  6.5 247.0 %reduce-scatter.2.cloned.1.call-start = ((), (), s32[]{:S(2)}) async-start(), calls=%async_computation.1 | async-start | bytes 4456448 | tf_op jit(solution)/shard_map/reduce_scatter | solution.py:133
  9.6 18.1 %collective-permute-start = (bf16[2,2,144,256]{3,2,1,0:T(8,128)(2,1)S(1)}, bf16[2,2,144,256]{3,2,1,0:T(8,128)(2,1)S(1)}, u32[]{:S(2)}, u32[]{:S(2)}) collective-permute-start(bf16[2,2,144,256]{3,2,1,0:T(8,128)(2,1)S(1)} %fusion.13), channel_id=1, source_target_pairs={{0,256},{16,272},{32,288},{48,304},{64,320},{80,336},{96,352},{112... | collective-permute-start | bytes 884744 | tf_op jit(solution)/shard_map/ppermute | solution.py:17
  27.9 24.0 %collective-permute-start.1 = (bf16[2,2,144,256]{3,2,1,0:T(8,128)(2,1)S(1)}, bf16[2,2,144,256]{3,2,1,0:T(8,128)(2,1)S(1)}, u32[]{:S(2)}, u32[]{:S(2)}) collective-permute-start(bf16[2,2,144,256]{3,2,1,0:T(8,128)(2,1)S(1)} %get-tuple-element.22), channel_id=1, source_target_pairs={{0,128},{16,144},{32,160},{48,176},{64,192},{80,208},{96,224},{112... | collective-permute-start | bytes 884744 | tf_op jit(solution)/shard_map/ppermute | solution.py:17
  52.1 10.4 %collective-permute-start.2 = (bf16[2,2,144,256]{3,2,1,0:T(8,128)(2,1)S(1)}, bf16[2,2,144,256]{3,2,1,0:T(8,128)(2,1)S(1)}, u32[]{:S(2)}, u32[]{:S(2)}) collective-permute-start(bf16[2,2,144,256]{3,2,1,0:T(8,128)(2,1)S(1)} %get-tuple-element.20), channel_id=1, source_target_pairs={{0,64},{16,80},{32,96},{48,112},{64,0},{80,16},{96,32},{112,48},{1... | collective-permute-start | bytes 884744 | tf_op jit(solution)/shard_map/ppermute | solution.py:17
  62.7 11.0 %collective-permute-start.3 = (bf16[2,2,144,256]{3,2,1,0:T(8,128)(2,1)S(1)}, bf16[2,2,144,256]{3,2,1,0:T(8,128)(2,1)S(1)}, u32[]{:S(2)}, u32[]{:S(2)}) collective-permute-start(bf16[2,2,144,256]{3,2,1,0:T(8,128)(2,1)S(1)} %get-tuple-element.18), channel_id=1, source_target_pairs={{0,32},{16,48},{32,0},{48,16},{64,96},{80,112},{96,64},{112,80},{1... | collective-permute-start | bytes 884744 | tf_op jit(solution)/shard_map/ppermute | solution.py:17
  74.0 3.5 %collective-permute-start.4 = (bf16[2,2,144,256]{3,2,1,0:T(8,128)(2,1)S(1)}, bf16[2,2,144,256]{3,2,1,0:T(8,128)(2,1)S(1)}, u32[]{:S(2)}, u32[]{:S(2)}) collective-permute-start(bf16[2,2,144,256]{3,2,1,0:T(8,128)(2,1)S(1)} %get-tuple-element.16), channel_id=1, source_target_pairs={{0,16},{16,0},{32,48},{48,32},{64,80},{80,64},{96,112},{112,96},{1... | collective-permute-start | bytes 884744 | tf_op jit(solution)/shard_map/ppermute | solution.py:17
  88.9 3.4 %collective-permute-start.5 = (bf16[2,2,128,256]{3,2,1,0:T(8,128)(2,1)S(1)}, bf16[2,2,128,256]{3,2,1,0:T(8,128)(2,1)S(1)}, u32[]{:S(2)}, u32[]{:S(2)}) collective-permute-start(bf16[2,2,128,256]{3,2,1,0:T(8,128)(2,1)S(1)} %fusion.12), channel_id=1, source_target_pairs={{0,16},{16,0},{32,48},{48,32},{64,80},{80,64},{96,112},{112,96},{1... | collective-permute-start | bytes 786440 | tf_op jit(solution)/shard_map/ppermute | solution.py:17
  92.6 11.7 %collective-permute-start.6 = (bf16[2,2,128,256]{3,2,1,0:T(8,128)(2,1)S(1)}, bf16[2,2,128,256]{3,2,1,0:T(8,128)(2,1)S(1)}, u32[]{:S(2)}, u32[]{:S(2)}) collective-permute-start(bf16[2,2,128,256]{3,2,1,0:T(8,128)(2,1)S(1)} %get-tuple-element.11), channel_id=1, source_target_pairs={{0,32},{16,48},{32,0},{48,16},{64,96},{80,112},{96,64},{112,80},{1... | collective-permute-start | bytes 786440 | tf_op jit(solution)/shard_map/ppermute | solution.py:17
  104.6 9.4 %collective-permute-start.7 = (bf16[2,2,128,256]{3,2,1,0:T(8,128)(2,1)S(1)}, bf16[2,2,128,256]{3,2,1,0:T(8,128)(2,1)S(1)}, u32[]{:S(2)}, u32[]{:S(2)}) collective-permute-start(bf16[2,2,128,256]{3,2,1,0:T(8,128)(2,1)S(1)} %get-tuple-element.9), channel_id=1, source_target_pairs={{0,64},{16,80},{32,96},{48,112},{64,0},{80,16},{96,32},{112,48},{1... | collective-permute-start | bytes 786440 | tf_op jit(solution)/shard_map/ppermute | solution.py:17
  114.1 23.5 %copy-start.1 = (bf16[256,256]{1,0:T(8,128)(2,1)S(1)}, bf16[256,256]{1,0:T(8,128)(2,1)}, u32[]{:S(2)}) copy-start(bf16[256,256]{1,0:T(8,128)(2,1)} %param.6) | copy-start | bytes 393220
  114.2 15.0 %collective-permute-start.8 = (bf16[2,2,128,256]{3,2,1,0:T(8,128)(2,1)S(1)}, bf16[2,2,128,256]{3,2,1,0:T(8,128)(2,1)S(1)}, u32[]{:S(2)}, u32[]{:S(2)}) collective-permute-start(bf16[2,2,128,256]{3,2,1,0:T(8,128)(2,1)S(1)} %get-tuple-element.7), channel_id=1, source_target_pairs={{0,128},{16,144},{32,160},{48,176},{64,192},{80,208},{96,224},{112... | collective-permute-start | bytes 786440 | tf_op jit(solution)/shard_map/ppermute | solution.py:17
  129.5 20.3 %copy-start.2 = (f32[256]{0:T(256)S(1)}, f32[256]{0:T(256)}, u32[]{:S(2)}) copy-start(f32[256]{0:T(256)} %param.10) | copy-start | bytes 3076
  129.5 19.9 %collective-permute-start.9 = (bf16[2,2,128,256]{3,2,1,0:T(8,128)(2,1)S(1)}, bf16[2,2,128,256]{3,2,1,0:T(8,128)(2,1)S(1)}, u32[]{:S(2)}, u32[]{:S(2)}) collective-permute-start(bf16[2,2,128,256]{3,2,1,0:T(8,128)(2,1)S(1)} %get-tuple-element.5), channel_id=1, source_target_pairs={{0,256},{16,272},{32,288},{48,304},{64,320},{80,336},{96,352},{112... | collective-permute-start | bytes 786440 | tf_op jit(solution)/shard_map/ppermute | solution.py:17
  137.7 12.2 %copy-start = (bf16[256,8192]{1,0:T(8,128)(2,1)S(1)}, bf16[256,8192]{1,0:T(8,128)(2,1)}, u32[]{:S(2)}) copy-start(bf16[256,8192]{1,0:T(8,128)(2,1)} %param.11) | copy-start | bytes 12582916
Sparse Core Ops, SparseCore 0:
  153.3 100.1 reduce-scatter.1
where the time goes:
time: 262 us; the launch traced here: 260 us
  waiting for transfers between devices  178 us (68%)
  starting transfers between devices  46.7 us (18%)
  between operations  15.4 us (6%)
  matrix products  14.3 us (5%)
  other arithmetic  3.76 us (1%)
    reduce_scatter x1, waiting for transfers between devices, body(): lax.psum_scatter(jnp.dot(gated, weight, preferred_element_type=jnp.float3...  100 us
    ppermute x10, waiting for transfers between devices, from_partner(): return lax.ppermute(value, axis, pairs)  77.7 us
    ppermute x10, starting transfers between devices, from_partner(): return lax.ppermute(value, axis, pairs)  46.7 us
  transfers between devices with their start and end apart: 11, of which 11 were waited for; matrix products, arithmetic and copies ran while one was open for 0% of the time, Pallas kernels for 0%

commit v1 on v0

v1 whole, which is shorter than its diff:
```python
import functools

import jax
import jax.numpy as jnp
from jax import lax
from jax.experimental import pallas as pl
from jax.experimental.pallas import tpu as pltpu
from jax.sharding import PartitionSpec as P

F32 = jnp.float32
BF16 = jnp.bfloat16
LANES = 128
SLAB = 8
BLOCK = 2 * LANES
UNROLL = 4
CHUNKS = 8


def remote(src, dst, send, recv, device):
    return pltpu.make_async_remote_copy(
        src_ref=src,
        dst_ref=dst,
        send_sem=send,
        recv_sem=recv,
        device_id=device,
        device_id_type=pl.DeviceIdType.MESH,
    )


def kernel(
    S, Y,
    query, key, value, filters, skip, weight, out,
    sx, rx, sf, rf, toeplitz, lhs, acc, sy, ry, gated, gated_x, wv, part, ss, sr, fo,
    x_send, x_recv, f_send, f_recv, y_send, y_recv, w_local, wd_send, wd_recv, wf_send, wf_recv,
    g_sem, r_send, r_recv, o_send, o_recv,
):
    seq = lax.axis_index("seq")
    ten = lax.axis_index("tensor")
    y = ten // 2
    xl = ten % 2
    core = seq % 2
    across = (seq, ten + 1 - 2 * xl)
    beside = (seq + 1 - 2 * core, ten)
    ahead = (seq, (ten + 2) % (2 * Y))
    behind = (seq, (ten + 2 * Y - 2) % (2 * Y))
    width = query.shape[1]
    columns = weight.shape[1]
    wide = columns // 2
    chunk = wide // CHUNKS
    half = CHUNKS // 2
    rows = BLOCK // Y

    barrier = pltpu.get_barrier_semaphore()

    def greet(device):
        pl.semaphore_signal(barrier, inc=1, device_id=device, device_id_type=pl.DeviceIdType.MESH)

    for device in (across, ahead, behind):
        greet(device)

    def greet_seq(d, _):
        greet(((seq + d) % S, ten))
        return 0

    lax.fori_loop(1, S, greet_seq, 0)

    def own_weight(j):
        return pltpu.make_async_copy(
            weight.at[:, pl.ds(pl.multiple_of(xl * wide + j * chunk, LANES), chunk)], wv.at[0, j], w_local.at[j]
        )

    for j in range(CHUNKS):
        own_weight(j).start()

    mixed = key[...].astype(F32) * value[...].astype(F32)
    turned = mixed.T
    sx[...] = jnp.concatenate(
        [turned[:, :LANES].reshape(S, SLAB, LANES), turned[:, LANES:].reshape(S, SLAB, LANES)], axis=1
    ).astype(BF16)
    for g in range(filters.shape[0]):
        for h in range(2):
            sf[g, h : h + 1, :] = filters[g : g + 1, h * LANES : (h + 1) * LANES]
    rx[pl.ds(seq, 1)] = sx[pl.ds(seq, 1)]
    rf[pl.ds(seq, 1)] = sf[pl.ds(seq // 2, 1)]

    pl.semaphore_wait(barrier, S + 2)

    def taps_copy(d):
        p = (seq + d) % S
        return remote(sf.at[p // 2], rf.at[seq], f_send.at[d], f_recv.at[d], (p, ten))

    def taps_wait(d):
        s = (seq + S - d) % S
        remote(sf.at[0], rf.at[s], f_send.at[d], f_recv.at[d], (s, ten)).wait_recv()

    def signal_copy(d):
        p = (seq + d) % S
        return remote(sx.at[p], rx.at[seq], x_send.at[d], x_recv.at[d], (p, ten))

    def signal_wait(d):
        s = (seq + S - d) % S
        remote(sx.at[s], rx.at[s], x_send.at[d], x_recv.at[d], (s, ten)).wait_recv()

    def response_copy(d):
        p = (seq + d) % S
        return remote(sy.at[p], ry.at[seq], y_send.at[d], y_recv.at[d], (p, ten))

    def response_wait(d):
        s = (seq + S - d) % S
        remote(sy.at[s], ry.at[s], y_send.at[d], y_recv.at[d], (s, ten)).wait_recv()

    def each(function):
        def step(d, _):
            function(d)
            return 0

        lax.fori_loop(1, S, step, 0)

    each(lambda d: taps_copy(d).start())
    each(lambda d: signal_copy(d).start())

    def direct(i):
        j = core * half + i
        return remote(
            weight.at[:, pl.ds(pl.multiple_of((1 - xl) * wide + j * chunk, LANES), chunk)],
            wv.at[1, j], wd_send.at[i], wd_recv.at[i], across,
        )

    def forward(i):
        j = core * half + i
        return remote(wv.at[1, j], wv.at[1, j], wf_send.at[i], wf_recv.at[i], beside)

    def forwarded(i):
        j = (1 - core) * half + i
        return remote(wv.at[1, j], wv.at[1, j], wf_send.at[i], wf_recv.at[i], beside)

    for i in range(half):
        direct(i).start()

    each(taps_wait)
    toeplitz[0, 1, :, 0:LANES] = jnp.zeros((LANES, LANES), BF16)
    lane = lax.broadcasted_iota(jnp.int32, (LANES, LANES), 1)
    down = lax.broadcasted_iota(jnp.int32, (LANES, LANES), 0)
    mask = lane >= down

    def build(a, before):
        for h in range(2):
            row = jnp.broadcast_to(rf[a, h : h + 1, :], (LANES, LANES))
            rolled = pltpu.roll(row, 0, 1, stride=1, stride_axis=0)
            block = jnp.where(mask, rolled, before).astype(BF16)
            before = rolled
            if h == 0:
                toeplitz[a, 0, :, 0:LANES] = block
                toeplitz[a, 1, :, LANES:BLOCK] = block
            else:
                toeplitz[a, 0, :, LANES:BLOCK] = block
                toeplitz[a + 1, 1, :, 0:LANES] = block
        return before

    lax.fori_loop(0, S, build, jnp.zeros((LANES, LANES), F32))

    each(signal_wait)
    signal = rx[...].astype(F32)
    for h in range(2):
        piece = signal[:, h * SLAB : (h + 1) * SLAB, :].reshape(S * SLAB, LANES)
        for r in range(UNROLL):
            shifted = piece
            if r > 0:
                shifted = jnp.concatenate([jnp.zeros((r * SLAB, LANES), F32), piece[: (S - r) * SLAB]], axis=0)
            lhs[:, r * BLOCK + h * LANES : r * BLOCK + (h + 1) * LANES] = shifted.astype(BF16)
    for step in range(S // UNROLL):
        top = step * UNROLL * SLAB
        taps = toeplitz[step * UNROLL : (step + 1) * UNROLL].reshape(UNROLL * BLOCK, BLOCK)
        product = jnp.dot(lhs[: S * SLAB - top, :], taps, preferred_element_type=F32)
        if step == 0:
            acc[...] = product
        else:
            acc[top:, :] += product
    sy[...] = jnp.concatenate(
        [acc[:, :LANES].reshape(S, SLAB, LANES), acc[:, LANES:].reshape(S, SLAB, LANES)], axis=1
    ).astype(BF16)
    each(lambda d: response_copy(d).start())
    ry[pl.ds(seq, 1)] = sy[pl.ds(seq, 1)]

    for i in range(half):
        direct(i).wait_recv()
        forward(i).start()

    each(response_wait)
    answer = ry[...].astype(F32)
    for h in range(2):
        span = slice(h * LANES, (h + 1) * LANES)
        response = answer[:, h * SLAB : (h + 1) * SLAB, :].reshape(width, LANES).T
        signal = key[span, :].astype(F32) * value[span, :].astype(F32)
        gated[span, :] = (query[span, :].astype(F32) * (response + skip[...] * signal)).astype(BF16)

    exchange = remote(gated, gated_x, g_sem.at[0], g_sem.at[1], across)
    exchange.start()
    for j in range(CHUNKS):
        own_weight(j).wait()
    exchange.wait_recv()

    steps = [((Y - 1) // 2, Y // 2), (Y // 2, (Y - 1) // 2)]

    def hop(i, slot, device):
        return remote(ss.at[i, slot], sr.at[i, slot], r_send.at[i, slot], r_recv.at[i, slot], device)

    def pairs(function):
        def step(pair, _):
            for parity in range(2):
                function(2 * pair + parity, *steps[parity])
            return 0

        lax.fori_loop(0, half, step, 0)

    def project(i, up, low):
        j = (core * half + i) % CHUNKS
        term = jnp.dot(gated[...], wv[0, j], preferred_element_type=F32)
        term = term + jnp.dot(gated_x[...], wv[1, j], preferred_element_type=F32)
        part[i] = term.reshape(Y, rows, chunk)
        advance(0, i, up, low)

    def advance(s, i, up, low):
        for slot, count, device, owner in (
            (0, up, ahead, (y + up - s) % Y),
            (up, low, behind, (y + Y - low + s) % Y),
        ):
            if s >= count:
                continue
            total = part[i, owner]
            if s > 0:
                hop(i, slot + s - 1, device).wait_recv()
                total = total + sr[i, slot + s - 1].astype(F32)
            ss[i, slot + s] = total.astype(BF16)
            hop(i, slot + s, device).start()

    def deliver(i):
        j = (core * half + i) % CHUNKS
        place = pl.ds(pl.multiple_of(xl * wide + j * chunk, LANES), chunk)
        return remote(fo.at[i], out.at[:, place], o_send.at[i], o_recv.at[i], across)

    def delivered(i):
        j = (core * half + i) % CHUNKS
        place = pl.ds(pl.multiple_of((1 - xl) * wide + j * chunk, LANES), chunk)
        return remote(fo.at[i], out.at[:, place], o_send.at[i], o_recv.at[i], across)

    def finish(i, up, low):
        j = (core * half + i) % CHUNKS
        total = part[i, y]
        for slot, count, device in ((0, up, ahead), (up, low, behind)):
            if count:
                hop(i, slot + count - 1, device).wait_recv()
                total = total + sr[i, slot + count - 1].astype(F32)
        mine = jnp.where(xl == 0, total[: rows // 2], total[rows // 2 :])
        other = jnp.where(xl == 0, total[rows // 2 :], total[: rows // 2])
        fo[i] = other.astype(BF16)
        deliver(i).start()
        out[:, pl.ds(pl.multiple_of(xl * wide + j * chunk, LANES), chunk)] = mine.astype(BF16)

    def first(i, up, low):
        project(i, up, low)

    def second(i, up, low):
        forwarded(i - half).wait_recv()
        project(i, up, low)

    for i in range(half):
        first(i, *steps[i % 2])
    for i in range(half, CHUNKS):
        second(i, *steps[i % 2])
    for s in range(1, Y // 2):
        pairs(functools.partial(advance, s))
    pairs(finish)

    def drain(i, up, low):
        delivered(i).wait_recv()
        deliver(i).wait_send()
        for slot in range(Y - 1):
            hop(i, slot, ahead).wait_send()

    pairs(drain)
    exchange.wait_send()
    for i in range(half):
        direct(i).wait_send()
        forward(i).wait_send()
    each(lambda d: taps_copy(d).wait_send())
    each(lambda d: signal_copy(d).wait_send())
    each(lambda d: response_copy(d).wait_send())


def body(query, key_branch, value, filters, skip, weight):
    S = lax.axis_size("seq")
    T = lax.axis_size("tensor")
    Y = T // 2
    width = query.shape[1]
    columns = weight.shape[1]
    chunk = columns // 2 // CHUNKS
    rows = BLOCK // Y
    vmem = pl.BlockSpec(memory_space=pltpu.VMEM)
    dma = pltpu.SemaphoreType.DMA
    slabs = pltpu.VMEM((S, 2 * SLAB, LANES), BF16)
    return pl.pallas_call(
        functools.partial(kernel, S, Y),
        out_shape=jax.ShapeDtypeStruct((BLOCK // T, columns), BF16),
        in_specs=[vmem] * 5 + [pl.BlockSpec(memory_space=pl.ANY)],
        out_specs=vmem,
        scratch_shapes=[
            slabs, slabs,
            pltpu.VMEM((filters.shape[0], 2, LANES), F32), pltpu.VMEM((S, 2, LANES), F32),
            pltpu.VMEM((S + 1, 2, LANES, BLOCK), BF16),
            pltpu.VMEM((S * SLAB, UNROLL * BLOCK), BF16),
            pltpu.VMEM((S * SLAB, BLOCK), F32),
            slabs, slabs,
            pltpu.VMEM((BLOCK, width), BF16), pltpu.VMEM((BLOCK, width), BF16),
            pltpu.VMEM((2, CHUNKS, width, chunk), BF16),
            pltpu.VMEM((CHUNKS, Y, rows, chunk), F32),
            pltpu.VMEM((CHUNKS, Y - 1, rows, chunk), BF16),
            pltpu.VMEM((CHUNKS, Y - 1, rows, chunk), BF16),
            pltpu.VMEM((CHUNKS, rows // 2, chunk), BF16),
            dma((S,)), dma((S,)), dma((S,)), dma((S,)), dma((S,)), dma((S,)),
            dma((CHUNKS,)),
            dma((CHUNKS // 2,)), dma((CHUNKS // 2,)), dma((CHUNKS // 2,)), dma((CHUNKS // 2,)),
            dma((2,)),
            dma((CHUNKS, Y - 1)), dma((CHUNKS, Y - 1)),
            dma((CHUNKS,)), dma((CHUNKS,)),
        ],
        compiler_params=pltpu.CompilerParams(
            collective_id=0, has_side_effects=True, vmem_limit_bytes=48 * 2**20
        ),
        name="hyena",
    )(query, key_branch, value, filters, skip.reshape(1, width), weight)


def solution(mesh):
    return jax.shard_map(
        body,
        mesh=mesh,
        in_specs=(
            P("seq", "tensor"),
            P("seq", "tensor"),
            P("seq", "tensor"),
            P("tensor", "seq"),
            P("tensor"),
            P("tensor", None),
        ),
        out_specs=P(("seq", "tensor"), None),
        check_vma=False,
    )
```

time: 262 us -> 84.4 us (0.32)
  waiting for transfers between devices: 178 us -> 0 us
  Pallas kernels: 0 us -> 77.1 us
  starting transfers between devices: 46.7 us -> 0 us
  between operations: 15.4 us -> 0.02 us
  matrix products: 14.3 us -> 0 us
  local copies, waits for them, and re-layouts: 2.17 us -> 7 us
  other arithmetic: 3.76 us -> 0 us
    reduce_scatter x1 -> x0, waiting for transfers between devices: 100 us -> none  [body(): lax.psum_scatter(jnp.dot(gated, weight, preferred_element_type=jnp.float3...]
    ppermute x10 -> x0, waiting for transfers between devices: 77.7 us -> none  [from_partner(): return lax.ppermute(value, axis, pairs)]
    pallas_call x0 -> x1, Pallas kernels: none -> 77.1 us  [body(): pl.pallas_call(functools.partial(kernel, S, Y), out_shape=jax.ShapeDtypeS...]
    ppermute x10 -> x0, starting transfers between devices: 46.7 us -> none  [from_partner(): return lax.ppermute(value, axis, pairs)]
    dot_general x9 -> x0, matrix products: 14.3 us -> none  [the longest x1 3.25 us: body(): jnp.dot(gated, weight, preferred_element_type=jnp.float32)]
    unnamed x9 -> x13, local copies, waits for them, and re-layouts: 2.13 us -> 7 us
  transfers between devices with their start and end apart: 11 -> 0, of which waited for: 11 -> 0; matrix products, arithmetic and copies ran while one was open for 0% -> 0% of each run, Pallas kernels for 0% -> 0%
where the time goes in v1:
time: 84.4 us; the launch traced here: 84.1 us
  Pallas kernels  77.1 us (91%)
  local copies, waits for them, and re-layouts  7 us (8%)
    pallas_call x1, Pallas kernels, body(): pl.pallas_call(functools.partial(kernel, S, Y), out_shape=jax.ShapeDtypeS...  77.1 us
    unnamed x13, local copies, waits for them, and re-layouts  7 us

profile of v1, /device:TPU:6, one launch (start us, length us, event | category | flops | bytes accessed | tf_op | source)
XLA Modules:
  0.0 84.1 jit_solution(3812086313822663551)
XLA Ops:
  0.0 0.0 copy-start
  0.0 2.2 %copy-done = bf16[256,8192]{1,0:T(8,128)(2,1)S(1)} copy-done((bf16[256,8192]{1,0:T(8,128)(2,1)S(1)}, bf16[256,8192]{1,0:T(8,128)(2,1)}, u32[]{:S(2)}) %copy-start) | copy-done | bytes 4194328
  2.2 0.0 copy-start.1
  2.2 0.9 %copy-done.1 = bf16[256,256]{1,0:T(8,128)(2,1)S(1)} copy-done((bf16[256,256]{1,0:T(8,128)(2,1)S(1)}, bf16[256,256]{1,0:T(8,128)(2,1)}, u32[]{:S(2)}) %copy-start.1) | copy-done | bytes 131096
  3.1 0.0 copy-start.2
  3.1 0.9 %copy-done.2 = bf16[256,256]{1,0:T(8,128)(2,1)S(1)} copy-done((bf16[256,256]{1,0:T(8,128)(2,1)S(1)}, bf16[256,256]{1,0:T(8,128)(2,1)}, u32[]{:S(2)}) %copy-start.2) | copy-done | bytes 131096
  4.0 0.0 copy-start.3
  4.0 0.9 %copy-done.3 = bf16[256,256]{1,0:T(8,128)(2,1)S(1)} copy-done((bf16[256,256]{1,0:T(8,128)(2,1)S(1)}, bf16[256,256]{1,0:T(8,128)(2,1)}, u32[]{:S(2)}) %copy-start.3) | copy-done | bytes 131096
  4.9 0.0 copy-start.4
  4.9 0.7 copy-done.4
  5.6 0.0 copy-start.5
  5.6 0.7 copy-done.5
  6.3 77.1 %hyena.1 = bf16[16,8192]{1,0:T(8,128)(2,1)S(1)} custom-call(bf16[256,256]{1,0:T(8,128)(2,1)S(1)} %copy-done.1, bf16[256,256]{1,0:T(8,128)(2,1)S(1)} %copy-done.2, bf16[256,256]{1,0:T(8,128)(2,1)S(1)} %copy-done.3, f32[16,256]{1,0:T(8,128)S(1)} %copy-done.4, f32[1,256]{1,0:T(1,128)S(1)} %bitcast.1, bf16[256,8192]{1,0:T(8,128)(2,1)S(1)} %copy-done), custom_call_target="tpu_custom_call" | custom-call | tf_op jit(solution)/shard_map/hyena/pallas_call | solution.py:302
  83.4 0.7 copy.8
Async XLA Ops:
  0.0 2.2 %copy-start = (bf16[256,8192]{1,0:T(8,128)(2,1)S(1)}, bf16[256,8192]{1,0:T(8,128)(2,1)}, u32[]{:S(2)}) copy-start(bf16[256,8192]{1,0:T(8,128)(2,1)} %weight.1) | copy-start | bytes 12582916
  2.2 0.9 %copy-start.1 = (bf16[256,256]{1,0:T(8,128)(2,1)S(1)}, bf16[256,256]{1,0:T(8,128)(2,1)}, u32[]{:S(2)}) copy-start(bf16[256,256]{1,0:T(8,128)(2,1)} %query.1) | copy-start | bytes 393220
  3.1 0.9 %copy-start.2 = (bf16[256,256]{1,0:T(8,128)(2,1)S(1)}, bf16[256,256]{1,0:T(8,128)(2,1)}, u32[]{:S(2)}) copy-start(bf16[256,256]{1,0:T(8,128)(2,1)} %key.1) | copy-start | bytes 393220
  4.0 0.9 %copy-start.3 = (bf16[256,256]{1,0:T(8,128)(2,1)S(1)}, bf16[256,256]{1,0:T(8,128)(2,1)}, u32[]{:S(2)}) copy-start(bf16[256,256]{1,0:T(8,128)(2,1)} %value.1) | copy-start | bytes 393220
  4.9 0.7 copy-start.4
  5.6 0.7 copy-start.5

commit v2 on v1

--- a/solution.py
+++ b/solution.py
@@ -29,10 +29,11 @@
 
 def kernel(
     S, Y,
-    query, key, value, filters, skip, weight, out,
-    sx, rx, sf, rf, toeplitz, lhs, acc, sy, ry, gated, gated_x, wv, part, ss, sr, fo,
-    x_send, x_recv, f_send, f_recv, y_send, y_recv, w_local, wd_send, wd_recv, wf_send, wf_recv,
-    g_sem, r_send, r_recv, o_send, o_recv,
+    query_in, key_in, value_in, filters_in, skip_in, weight, out,
+    query, key, value, filters, skip, i_sem,
+    sx, rx, sq, rq, sf, rf, toeplitz, lhs, acc, sg, rg, gated, wv, part, ss, sr, fo,
+    x_send, x_recv, q_send, q_recv, f_send, f_recv, g_send, g_recv,
+    w_local, wd_send, wd_recv, wf_send, wf_recv, r_send, r_recv, o_send, o_recv,
 ):
     seq = lax.axis_index("seq")
     ten = lax.axis_index("tensor")
@@ -40,6 +41,7 @@
     xl = ten % 2
     core = seq % 2
     across = (seq, ten + 1 - 2 * xl)
+    around = (seq + 2 - 4 * (seq // 2 % 2), ten + 1 - 2 * xl)
     beside = (seq + 1 - 2 * core, ten)
     ahead = (seq, (ten + 2) % (2 * Y))
     behind = (seq, (ten + 2 * Y - 2) % (2 * Y))
@@ -50,12 +52,21 @@
     half = CHUNKS // 2
     rows = BLOCK // Y
 
+    inputs = [
+        pltpu.make_async_copy(source, target, i_sem.at[n])
+        for n, (source, target) in enumerate(
+            ((key_in, key), (value_in, value), (filters_in, filters), (query_in, query), (skip_in, skip))
+        )
+    ]
+    for copy in inputs:
+        copy.start()
+
     barrier = pltpu.get_barrier_semaphore()
 
     def greet(device):
         pl.semaphore_signal(barrier, inc=1, device_id=device, device_id_type=pl.DeviceIdType.MESH)
 
-    for device in (across, ahead, behind):
+    for device in (across, around, ahead, behind):
         greet(device)
 
     def greet_seq(d, _):
@@ -72,18 +83,23 @@
     for j in range(CHUNKS):
         own_weight(j).start()
 
-    mixed = key[...].astype(F32) * value[...].astype(F32)
-    turned = mixed.T
-    sx[...] = jnp.concatenate(
-        [turned[:, :LANES].reshape(S, SLAB, LANES), turned[:, LANES:].reshape(S, SLAB, LANES)], axis=1
-    ).astype(BF16)
+    for copy in inputs:
+        copy.wait()
+
+    def slabs(array):
+        turned = array.T
+        return jnp.concatenate(
+            [turned[:, :LANES].reshape(S, SLAB, LANES), turned[:, LANES:].reshape(S, SLAB, LANES)], axis=1
+        ).astype(BF16)
+
+    sx[...] = slabs(key[...].astype(F32) * value[...].astype(F32))
     for g in range(filters.shape[0]):
         for h in range(2):
             sf[g, h : h + 1, :] = filters[g : g + 1, h * LANES : (h + 1) * LANES]
     rx[pl.ds(seq, 1)] = sx[pl.ds(seq, 1)]
     rf[pl.ds(seq, 1)] = sf[pl.ds(seq // 2, 1)]
 
-    pl.semaphore_wait(barrier, S + 2)
+    pl.semaphore_wait(barrier, S + 3)
 
     def taps_copy(d):
         p = (seq + d) % S
@@ -101,13 +117,23 @@
         s = (seq + S - d) % S
         remote(sx.at[s], rx.at[s], x_send.at[d], x_recv.at[d], (s, ten)).wait_recv()
 
-    def response_copy(d):
+    def query_copy(d):
         p = (seq + d) % S
-        return remote(sy.at[p], ry.at[seq], y_send.at[d], y_recv.at[d], (p, ten))
-
-    def response_wait(d):
+        return remote(sq.at[p], rq.at[seq], q_send.at[d], q_recv.at[d], (p, ten))
+
+    def query_wait(d):
         s = (seq + S - d) % S
-        remote(sy.at[s], ry.at[s], y_send.at[d], y_recv.at[d], (s, ten)).wait_recv()
+        remote(sq.at[s], rq.at[s], q_send.at[d], q_recv.at[d], (s, ten)).wait_recv()
+
+    def gated_copy(d, side):
+        p = (seq + d) % S
+        device = (p, ten) if side == 0 else (p, ten + 1 - 2 * xl)
+        return remote(sg.at[p], rg.at[side, seq], g_send.at[side, d], g_recv.at[side, d], device)
+
+    def gated_wait(d, side):
+        s = (seq + S - d) % S
+        device = (s, ten) if side == 0 else (s, ten + 1 - 2 * xl)
+        remote(sg.at[s], rg.at[side, s], g_send.at[side, d], g_recv.at[side, d], device).wait_recv()
 
     def each(function):
         def step(d, _):
@@ -118,12 +144,15 @@
 
     each(lambda d: taps_copy(d).start())
     each(lambda d: signal_copy(d).start())
+    sq[...] = slabs(query[...].astype(F32))
+    rq[pl.ds(seq, 1)] = sq[pl.ds(seq, 1)]
+    each(lambda d: query_copy(d).start())
 
     def direct(i):
         j = core * half + i
         return remote(
             weight.at[:, pl.ds(pl.multiple_of((1 - xl) * wide + j * chunk, LANES), chunk)],
-            wv.at[1, j], wd_send.at[i], wd_recv.at[i], across,
+            wv.at[1, j], wd_send.at[i], wd_recv.at[i], across if i % 2 == 0 else around,
         )
 
     def forward(i):
@@ -157,7 +186,7 @@
                 toeplitz[a + 1, 1, :, 0:LANES] = block
         return before
 
-    lax.fori_loop(0, S, build, jnp.zeros((LANES, LANES), F32))
+    lax.fori_loop(0, S, build, jnp.zeros((LANES, LANES), F32), unroll=4)
 
     each(signal_wait)
     signal = rx[...].astype(F32)
@@ -176,51 +205,71 @@
             acc[...] = product
         else:
             acc[top:, :] += product
-    sy[...] = jnp.concatenate(
-        [acc[:, :LANES].reshape(S, SLAB, LANES), acc[:, LANES:].reshape(S, SLAB, LANES)], axis=1
-    ).astype(BF16)
-    each(lambda d: response_copy(d).start())
-    ry[pl.ds(seq, 1)] = sy[pl.ds(seq, 1)]
-
-    for i in range(half):
+    each(query_wait)
+    spot = lax.broadcasted_iota(jnp.int32, (SLAB, width), 1) - SLAB * seq
+    picked = spot == lax.broadcasted_iota(jnp.int32, (SLAB, width), 0)
+    direct_term = jnp.sum(jnp.where(picked, skip[...], 0.0), axis=1, keepdims=True)
+    pieces = []
+    for h in range(2):
+        span = slice(h * SLAB, (h + 1) * SLAB)
+        response = acc[:, h * LANES : (h + 1) * LANES].reshape(S, SLAB, LANES)
+        term = response + direct_term[None] * rx[...].astype(F32)[:, span]
+        pieces.append(rq[...].astype(F32)[:, span] * term)
+    sg[...] = jnp.concatenate(pieces, axis=1).astype(BF16)
+
+    def send_gated(d):
+        gated_copy(d, 0).start()
+        gated_copy(d, 1).start()
+
+    each(send_gated)
+    gated_copy(0, 1).start()
+    rg[0, pl.ds(seq, 1)] = sg[pl.ds(seq, 1)]
+
+    for i in range(half // 2):
         direct(i).wait_recv()
         forward(i).start()
-
-    each(response_wait)
-    answer = ry[...].astype(F32)
-    for h in range(2):
-        span = slice(h * LANES, (h + 1) * LANES)
-        response = answer[:, h * SLAB : (h + 1) * SLAB, :].reshape(width, LANES).T
-        signal = key[span, :].astype(F32) * value[span, :].astype(F32)
-        gated[span, :] = (query[span, :].astype(F32) * (response + skip[...] * signal)).astype(BF16)
-
-    exchange = remote(gated, gated_x, g_sem.at[0], g_sem.at[1], across)
-    exchange.start()
     for j in range(CHUNKS):
         own_weight(j).wait()
-    exchange.wait_recv()
+
+    def wait_gated(d):
+        gated_wait(d, 0)
+        gated_wait(d, 1)
+
+    each(wait_gated)
+    gated_wait(0, 1)
+    for side in range(2):
+        for h in range(2):
+            piece = rg[side].astype(F32)[:, h * SLAB : (h + 1) * SLAB].reshape(width, LANES)
+            gated[side, h * LANES : (h + 1) * LANES, :] = piece.T.astype(BF16)
+    for i in range(half // 2, half):
+        direct(i).wait_recv()
+        forward(i).start()
 
     steps = [((Y - 1) // 2, Y // 2), (Y // 2, (Y - 1) // 2)]
 
     def hop(i, slot, device):
         return remote(ss.at[i, slot], sr.at[i, slot], r_send.at[i, slot], r_recv.at[i, slot], device)
+
+    def chunk_of(i, parity):
+        return (core + parity) % 2 * half + i // 2
 
     def pairs(function):
         def step(pair, _):
             for parity in range(2):
-                function(2 * pair + parity, *steps[parity])
+                function(2 * pair + parity, parity)
             return 0
 
         lax.fori_loop(0, half, step, 0)
 
-    def project(i, up, low):
-        j = (core * half + i) % CHUNKS
-        term = jnp.dot(gated[...], wv[0, j], preferred_element_type=F32)
-        term = term + jnp.dot(gated_x[...], wv[1, j], preferred_element_type=F32)
+    def project(i, parity):
+        j = chunk_of(i, parity)
+        term = jnp.dot(gated[0], wv[0, j], preferred_element_type=F32)
+        term = term + jnp.dot(gated[1], wv[1, j], preferred_element_type=F32)
         part[i] = term.reshape(Y, rows, chunk)
-        advance(0, i, up, low)
-
-    def advance(s, i, up, low):
+        advance(0, i, parity)
+
+    def advance(s, i, parity):
+        up, low = steps[parity]
         for slot, count, device, owner in (
             (0, up, ahead, (y + up - s) % Y),
             (up, low, behind, (y + Y - low + s) % Y),
@@ -234,18 +283,19 @@
             ss[i, slot + s] = total.astype(BF16)
             hop(i, slot + s, device).start()
 
-    def deliver(i):
-        j = (core * half + i) % CHUNKS
+    def deliver(i, parity):
+        j = chunk_of(i, parity)
         place = pl.ds(pl.multiple_of(xl * wide + j * chunk, LANES), chunk)
         return remote(fo.at[i], out.at[:, place], o_send.at[i], o_recv.at[i], across)
 
-    def delivered(i):
-        j = (core * half + i) % CHUNKS
+    def delivered(i, parity):
+        j = chunk_of(i, parity)
         place = pl.ds(pl.multiple_of((1 - xl) * wide + j * chunk, LANES), chunk)
         return remote(fo.at[i], out.at[:, place], o_send.at[i], o_recv.at[i], across)
 
-    def finish(i, up, low):
-        j = (core * half + i) % CHUNKS
+    def finish(i, parity):
+        up, low = steps[parity]
+        j = chunk_of(i, parity)
         total = part[i, y]
         for slot, count, device in ((0, up, ahead), (up, low, behind)):
             if count:
@@ -254,38 +304,34 @@
         mine = jnp.where(xl == 0, total[: rows // 2], total[rows // 2 :])
         other = jnp.where(xl == 0, total[rows // 2 :], total[: rows // 2])
         fo[i] = other.astype(BF16)
-        deliver(i).start()
+        deliver(i, parity).start()
         out[:, pl.ds(pl.multiple_of(xl * wide + j * chunk, LANES), chunk)] = mine.astype(BF16)
 
-    def first(i, up, low):
-        project(i, up, low)
-
-    def second(i, up, low):
-        forwarded(i - half).wait_recv()
-        project(i, up, low)
-
-    for i in range(half):
-        first(i, *steps[i % 2])
-    for i in range(half, CHUNKS):
-        second(i, *steps[i % 2])
+    for i in range(CHUNKS):
+        if i % 2 == 1:
+            forwarded(i // 2).wait_recv()
+        project(i, i % 2)
+    each(lambda d: taps_copy(d).wait_send())
+    each(lambda d: signal_copy(d).wait_send())
+    each(lambda d: query_copy(d).wait_send())
     for s in range(1, Y // 2):
         pairs(functools.partial(advance, s))
+        if s == 1:
+            each(lambda d: gated_copy(d, 0).wait_send())
+            each(lambda d: gated_copy(d, 1).wait_send())
+            gated_copy(0, 1).wait_send()
     pairs(finish)
 
-    def drain(i, up, low):
-        delivered(i).wait_recv()
-        deliver(i).wait_send()
+    def drain(i, parity):
+        delivered(i, parity).wait_recv()
+        deliver(i, parity).wait_send()
         for slot in range(Y - 1):
             hop(i, slot, ahead).wait_send()
 
     pairs(drain)
-    exchange.wait_send()
     for i in range(half):
         direct(i).wait_send()
         forward(i).wait_send()
-    each(lambda d: taps_copy(d).wait_send())
-    each(lambda d: signal_copy(d).wait_send())
-    each(lambda d: response_copy(d).wait_send())
 
 
 def body(query, key_branch, value, filters, skip, weight):
@@ -298,34 +344,35 @@
     rows = BLOCK // Y
     vmem = pl.BlockSpec(memory_space=pltpu.VMEM)
     dma = pltpu.SemaphoreType.DMA
-    slabs = pltpu.VMEM((S, 2 * SLAB, LANES), BF16)
+    slab = pltpu.VMEM((S, 2 * SLAB, LANES), BF16)
     return pl.pallas_call(
         functools.partial(kernel, S, Y),
         out_shape=jax.ShapeDtypeStruct((BLOCK // T, columns), BF16),
-        in_specs=[vmem] * 5 + [pl.BlockSpec(memory_space=pl.ANY)],
+        in_specs=[pl.BlockSpec(memory_space=pltpu.HBM)] * 6,
         out_specs=vmem,
         scratch_shapes=[
-            slabs, slabs,
+            pltpu.VMEM(query.shape, BF16), pltpu.VMEM(query.shape, BF16), pltpu.VMEM(query.shape, BF16),
+            pltpu.VMEM(filters.shape, F32), pltpu.VMEM((1, width), F32), dma((5,)),
+            slab, slab, slab, slab,
             pltpu.VMEM((filters.shape[0], 2, LANES), F32), pltpu.VMEM((S, 2, LANES), F32),
             pltpu.VMEM((S + 1, 2, LANES, BLOCK), BF16),
             pltpu.VMEM((S * SLAB, UNROLL * BLOCK), BF16),
             pltpu.VMEM((S * SLAB, BLOCK), F32),
-            slabs, slabs,
-            pltpu.VMEM((BLOCK, width), BF16), pltpu.VMEM((BLOCK, width), BF16),
+            slab, pltpu.VMEM((2, S, 2 * SLAB, LANES), BF16),
+            pltpu.VMEM((2, BLOCK, width), BF16),
             pltpu.VMEM((2, CHUNKS, width, chunk), BF16),
             pltpu.VMEM((CHUNKS, Y, rows, chunk), F32),
             pltpu.VMEM((CHUNKS, Y - 1, rows, chunk), BF16),
             pltpu.VMEM((CHUNKS, Y - 1, rows, chunk), BF16),
             pltpu.VMEM((CHUNKS, rows // 2, chunk), BF16),
-            dma((S,)), dma((S,)), dma((S,)), dma((S,)), dma((S,)), dma((S,)),
+            dma((S,)), dma((S,)), dma((S,)), dma((S,)), dma((S,)), dma((S,)), dma((2, S)), dma((2, S)),
             dma((CHUNKS,)),
             dma((CHUNKS // 2,)), dma((CHUNKS // 2,)), dma((CHUNKS // 2,)), dma((CHUNKS // 2,)),
-            dma((2,)),
             dma((CHUNKS, Y - 1)), dma((CHUNKS, Y - 1)),
             dma((CHUNKS,)), dma((CHUNKS,)),
         ],
         compiler_params=pltpu.CompilerParams(
-            collective_id=0, has_side_effects=True, vmem_limit_bytes=48 * 2**20
+            collective_id=0, has_side_effects=True, vmem_limit_bytes=60 * 2**20
         ),
         name="hyena",
     )(query, key_branch, value, filters, skip.reshape(1, width), weight)

time: 84.4 us -> 68.9 us (0.82)
  the two profiles are of different devices: /device:TPU:6 before, /device:TPU:2 now
where the time goes in v2:
time: 68.9 us; the launch traced here: 68.7 us
  Pallas kernels  67 us (97%)
  local copies, waits for them, and re-layouts  1.67 us (2%)
    pallas_call x1, Pallas kernels, body(): pl.pallas_call(functools.partial(kernel, S, Y), out_shape=jax.ShapeDtypeS...  67 us
    unnamed x1, local copies, waits for them, and re-layouts  1.67 us

profile of v2, /device:TPU:2, one launch (start us, length us, event | category | flops | bytes accessed | tf_op | source)
XLA Modules:
  0.0 68.7 jit_solution(6935305446814034367)
XLA Ops:
  0.0 67.0 %hyena.1 = bf16[16,8192]{1,0:T(8,128)(2,1)} custom-call(bf16[256,256]{1,0:T(8,128)(2,1)} %query_in.1, bf16[256,256]{1,0:T(8,128)(2,1)} %key_in.1, bf16[256,256]{1,0:T(8,128)(2,1)} %value_in.1, f32[16,256]{1,0:T(8,128)} %filters_in.1, f32[1,256]{1,0:T(1,128)} %bitcast.1, bf16[256,8192]{1,0:T(8,128)(2,1)} %weight.1), custom_call_target="tpu_custom_call" | custom-call | tf_op jit(solution)/shard_map/hyena/pallas_call | solution.py:348
  67.0 1.7 %copy.8 = bf16[16,8192]{1,0:T(8,128)(2,1)} copy(bf16[16,8192]{1,0:T(8,128)(2,1)} %hyena.1) | data formatting | bytes 524288

commit v3 on v2

v3 whole, which is shorter than its diff:
```python
import functools

import jax
import jax.numpy as jnp
from jax import lax
from jax.experimental import pallas as pl
from jax.experimental.pallas import tpu as pltpu
from jax.sharding import PartitionSpec as P

F32 = jnp.float32
BF16 = jnp.bfloat16
LANES = 128
GROUPS_OF_SLABS = 4
SLAB = 8
BLOCK = 2 * LANES
UNROLL = 4
CHUNKS = 8


def remote(src, dst, send, recv, device):
    return pltpu.make_async_remote_copy(
        src_ref=src,
        dst_ref=dst,
        send_sem=send,
        recv_sem=recv,
        device_id=device,
        device_id_type=pl.DeviceIdType.MESH,
    )


def kernel(
    S, Y,
    query_in, key_in, value_in, filters_in, skip_in, weight, out,
    factors, filters, skip, i_sem,
    sx, rx, sq, sf, rf, toeplitz, lhs, acc, sg, rg, gk, gx, gs, gated, wv, part, ss, sr, fo,
    x_send, x_recv, f_send, f_recv, g_send, g_recv, e_send, e_recv,
    w_local, wd_send, wd_recv, wf_send, wf_recv, r_send, r_recv, o_send, o_recv,
):
    seq = lax.axis_index("seq")
    ten = lax.axis_index("tensor")
    y = ten // 2
    xl = ten % 2
    core = seq % 2
    across = (seq, ten + 1 - 2 * xl)
    around = (seq + 2 - 4 * (seq // 2 % 2), ten + 1 - 2 * xl)
    beside = (seq + 1 - 2 * core, ten)
    ahead = (seq, (ten + 2) % (2 * Y))
    behind = (seq, (ten + 2 * Y - 2) % (2 * Y))
    width = factors.shape[2]
    columns = weight.shape[1]
    wide = columns // 2
    chunk = wide // CHUNKS
    half = CHUNKS // 2
    rows = BLOCK // Y
    group = S // GROUPS_OF_SLABS

    inputs = [
        pltpu.make_async_copy(key_in, factors.at[0], i_sem.at[0]),
        pltpu.make_async_copy(value_in, factors.at[1], i_sem.at[0]),
        pltpu.make_async_copy(query_in, factors.at[2], i_sem.at[0]),
        pltpu.make_async_copy(filters_in, filters, i_sem.at[1]),
        pltpu.make_async_copy(skip_in, skip, i_sem.at[2]),
    ]
    for copy in inputs:
        copy.start()

    barrier = pltpu.get_barrier_semaphore()

    def greet(device):
        pl.semaphore_signal(barrier, inc=1, device_id=device, device_id_type=pl.DeviceIdType.MESH)

    for device in (across, around, ahead, behind):
        greet(device)

    def greet_seq(d, _):
        greet(((seq + d) % S, ten))
        return 0

    lax.fori_loop(1, S, greet_seq, 0)

    def own_weight(j):
        return pltpu.make_async_copy(
            weight.at[:, pl.ds(pl.multiple_of(xl * wide + j * chunk, LANES), chunk)], wv.at[0, j], w_local.at[0]
        )

    for j in range(CHUNKS):
        own_weight(j).start()

    pltpu.make_async_copy(factors, factors, i_sem.at[0]).wait()
    inputs[3].wait()
    inputs[4].wait()

    def slabs(array):
        turned = array.T
        return jnp.concatenate(
            [turned[:, :LANES].reshape(S, SLAB, LANES), turned[:, LANES:].reshape(S, SLAB, LANES)], axis=1
        ).astype(BF16)

    sx[...] = slabs(factors[0].astype(F32) * factors[1].astype(F32))
    for g in range(filters.shape[0]):
        for h in range(2):
            sf[g, h : h + 1, :] = filters[g : g + 1, h * LANES : (h + 1) * LANES]
    rx[pl.ds(seq, 1)] = sx[pl.ds(seq, 1)]
    rf[pl.ds(seq, 1)] = sf[pl.ds(seq // 2, 1)]

    pl.semaphore_wait(barrier, S + 3)

    def taps_copy(k):
        p = (seq + S - k) % S
        return remote(sf.at[p // 2], rf.at[seq], f_send.at[0], f_recv.at[0], (p, ten))

    def signal_copy(k):
        p = (seq + S - k) % S
        return remote(sx.at[p], rx.at[seq], x_send.at[0], x_recv.at[0], (p, ten))

    def response_copy(k):
        p = (seq + S - k) % S
        return remote(sg.at[p], rg.at[k], g_send.at[0], g_recv.at[k // group], (p, ten))

    def relay(n):
        span = pl.ds(n * group, group)
        return remote(gk.at[span], gx.at[span], e_send.at[0], e_recv.at[n], across)

    order = [GROUPS_OF_SLABS // 2, GROUPS_OF_SLABS // 2 - 1] + list(range(GROUPS_OF_SLABS // 2 + 1, GROUPS_OF_SLABS)) + [0]

    def each_of(n, function):
        def step(k, _):
            function(k)
            return 0

        lax.fori_loop(max(n * group, 1), (n + 1) * group, step, 0)

    def each(function):
        for n in order:
            each_of(n, function)

    each(lambda k: taps_copy(k).start())
    each(lambda k: signal_copy(k).start())
    sq[...] = slabs(factors[2].astype(F32))

    def direct(i):
        j = core * half + i
        return remote(
            weight.at[:, pl.ds(pl.multiple_of((1 - xl) * wide + j * chunk, LANES), chunk)],
            wv.at[1, j], wd_send.at[0], wd_recv.at[i], across if i % 2 == 0 else around,
        )

    def forward(i):
        j = core * half + i
        return remote(wv.at[1, j], wv.at[1, j], wf_send.at[0], wf_recv.at[i], beside)

    def forwarded(i):
        j = (1 - core) * half + i
        return remote(wv.at[1, j], wv.at[1, j], wf_send.at[0], wf_recv.at[i], beside)

    for i in range(half):
        direct(i).start()

    everyone = pl.ds(0, S - 1)
    all_taps = remote(rf.at[everyone], rf.at[everyone], f_send.at[0], f_recv.at[0], across)
    all_signals = remote(rx.at[everyone], rx.at[everyone], x_send.at[0], x_recv.at[0], across)
    all_responses = remote(sg.at[everyone], rg.at[everyone], g_send.at[0], g_recv.at[0], across)
    all_relays = remote(gk, gx, e_send.at[0], e_recv.at[0], across)

    def some_responses(n):
        span = pl.ds(0, group if n > 0 else group - 1)
        return remote(sg.at[span], rg.at[span], g_send.at[0], g_recv.at[n], across)

    all_taps.wait_recv()
    toeplitz[0, 1, :, 0:LANES] = jnp.zeros((LANES, LANES), BF16)
    lane = lax.broadcasted_iota(jnp.int32, (LANES, LANES), 1)
    down = lax.broadcasted_iota(jnp.int32, (LANES, LANES), 0)
    mask = lane >= down

    def build(a, before):
        for h in range(2):
            row = jnp.broadcast_to(rf[a, h : h + 1, :], (LANES, LANES))
            rolled = pltpu.roll(row, 0, 1, stride=1, stride_axis=0)
            block = jnp.where(mask, rolled, before).astype(BF16)
            before = rolled
            if h == 0:
                toeplitz[a, 0, :, 0:LANES] = block
                toeplitz[a, 1, :, LANES:BLOCK] = block
            else:
                toeplitz[a, 0, :, LANES:BLOCK] = block
                toeplitz[a + 1, 1, :, 0:LANES] = block
        return before

    lax.fori_loop(0, S, build, jnp.zeros((LANES, LANES), F32), unroll=4)

    all_signals.wait_recv()
    signal = rx[...].astype(F32)
    for h in range(2):
        piece = signal[:, h * SLAB : (h + 1) * SLAB, :].reshape(S * SLAB, LANES)
        for r in range(UNROLL):
            shifted = piece
            if r > 0:
                shifted = jnp.concatenate([jnp.zeros((r * SLAB, LANES), F32), piece[: (S - r) * SLAB]], axis=0)
            lhs[:, r * BLOCK + h * LANES : r * BLOCK + (h + 1) * LANES] = shifted.astype(BF16)
    for step in range(S // UNROLL):
        top = step * UNROLL * SLAB
        taps = toeplitz[step * UNROLL : (step + 1) * UNROLL].reshape(UNROLL * BLOCK, BLOCK)
        product = jnp.dot(lhs[: S * SLAB - top, :], taps, preferred_element_type=F32)
        if step == 0:
            acc[...] = product
        else:
            acc[top:, :] += product
    spot = lax.broadcasted_iota(jnp.int32, (SLAB, width), 1) - SLAB * seq
    picked = spot == lax.broadcasted_iota(jnp.int32, (SLAB, width), 0)
    scale = jnp.sum(jnp.where(picked, skip[...], 0.0), axis=1, keepdims=True)
    pieces = []
    for h in range(2):
        response = acc[:, h * LANES : (h + 1) * LANES].reshape(S, SLAB, LANES)
        pieces.append(response + scale[None] * rx[...].astype(F32)[:, h * SLAB : (h + 1) * SLAB])
    sg[...] = jnp.concatenate(pieces, axis=1).astype(BF16)
    each(lambda k: response_copy(k).start())
    rg[pl.ds(0, 1)] = sg[pl.ds(seq, 1)]

    for i in range(half // 2):
        direct(i).wait_recv()
        forward(i).start()
    pltpu.make_async_copy(wv.at[0], wv.at[0], w_local.at[0]).wait()

    def turn(side):
        for h in range(2):
            piece = gs[...].astype(F32)[:, h * SLAB : (h + 1) * SLAB].reshape(width, LANES)
            gated[side, h * LANES : (h + 1) * LANES, :] = piece.T.astype(BF16)

    for n in order:
        some_responses(n).wait_recv()
        for k in range(n * group, (n + 1) * group):
            s = (seq + k) % S
            slab = (sq[s].astype(F32) * rg[k].astype(F32)).astype(BF16)
            gk[k] = slab
            gs[s] = slab
        relay(n).start()
    turn(0)

    def chunk_of(i, parity):
        return (core + parity) % 2 * half + i // 2

    for i in range(CHUNKS):
        term = jnp.dot(gated[0], wv[0, chunk_of(i, i % 2)], preferred_element_type=F32)
        part[i] = term.reshape(Y, rows, chunk)
    for n in order:
        relay(n).wait_recv()
    for k in range(S):
        gs[(seq + k) % S] = gx[k]
    turn(1)

    steps = [((Y - 1) // 2, Y // 2), (Y // 2, (Y - 1) // 2)]

    def hop(i, slot, device):
        return remote(ss.at[i, slot], sr.at[i, slot], r_send.at[0], r_recv.at[i, slot], device)

    def pairs(batch, function):
        def step(pair, _):
            for parity in range(2):
                function(2 * pair + parity, parity)
            return 0

        lax.fori_loop(batch * half // 2, (batch + 1) * half // 2, step, 0)

    def project(i, parity):
        j = chunk_of(i, parity)
        term = jnp.dot(gated[1], wv[1, j], preferred_element_type=F32)
        part[i] += term.reshape(Y, rows, chunk)
        advance(0, i, parity)

    def advance(s, i, parity):
        up, low = steps[parity]
        for slot, count, device, owner in (
            (0, up, ahead, (y + up - s) % Y),
            (up, low, behind, (y + Y - low + s) % Y),
        ):
            if s >= count:
                continue
            total = part[i, owner]
            if s > 0:
                hop(i, slot + s - 1, device).wait_recv()
                total = total + sr[i, slot + s - 1].astype(F32)
            ss[i, slot + s] = total.astype(BF16)
            hop(i, slot + s, device).start()

    def deliver(i, parity):
        j = chunk_of(i, parity)
        place = pl.ds(pl.multiple_of(xl * wide + j * chunk, LANES), chunk)
        return remote(fo.at[i], out.at[:, place], o_send.at[0], o_recv.at[0], across)

    def finish(i, parity):
        up, low = steps[parity]
        j = chunk_of(i, parity)
        total = part[i, y]
        for slot, count, device in ((0, up, ahead), (up, low, behind)):
            if count:
                hop(i, slot + count - 1, device).wait_recv()
                total = total + sr[i, slot + count - 1].astype(F32)
        mine = jnp.where(xl == 0, total[: rows // 2], total[rows // 2 :])
        other = jnp.where(xl == 0, total[rows // 2 :], total[: rows // 2])
        fo[i] = other.astype(BF16)
        deliver(i, parity).start()
        out[:, pl.ds(pl.multiple_of(xl * wide + j * chunk, LANES), chunk)] = mine.astype(BF16)

    for i in range(half):
        if i % 2 == 1:
            forwarded(i // 2).wait_recv()
        project(i, i % 2)
    all_taps.wait_send()
    all_signals.wait_send()
    all_responses.wait_send()
    all_relays.wait_send()
    for n in range(half // 2, half):
        direct(n).wait_recv()
        forward(n).start()
    pairs(0, functools.partial(advance, 1))
    for i in range(half, CHUNKS):
        if i % 2 == 1:
            forwarded(i // 2).wait_recv()
        project(i, i % 2)
    for s in range(2, Y // 2):
        pairs(0, functools.partial(advance, s))
        pairs(1, functools.partial(advance, s - 1))
    pairs(0, finish)
    if Y // 2 > 1:
        pairs(1, functools.partial(advance, Y // 2 - 1))
    pairs(1, finish)

    remote(wv.at[0, pl.ds(0, half)], wv.at[0, pl.ds(0, half)], wd_send.at[0], wd_recv.at[0], across).wait_send()
    remote(wv.at[1, pl.ds(0, half)], wv.at[1, pl.ds(0, half)], wf_send.at[0], wf_recv.at[0], beside).wait_send()
    remote(ss, sr, r_send.at[0], r_recv.at[0, 0], ahead).wait_send()
    other = out.at[:, pl.ds(pl.multiple_of((1 - xl) * wide, LANES), wide)]
    delivered = remote(other, other, o_send.at[0], o_recv.at[0], across)
    delivered.wait_send()
    delivered.wait_recv()


def body(query, key_branch, value, filters, skip, weight):
    S = lax.axis_size("seq")
    T = lax.axis_size("tensor")
    Y = T // 2
    width = query.shape[1]
    columns = weight.shape[1]
    chunk = columns // 2 // CHUNKS
    rows = BLOCK // Y
    vmem = pl.BlockSpec(memory_space=pltpu.VMEM)
    dma = pltpu.SemaphoreType.DMA
    slab = pltpu.VMEM((S, 2 * SLAB, LANES), BF16)
    return pl.pallas_call(
        functools.partial(kernel, S, Y),
        out_shape=jax.ShapeDtypeStruct((BLOCK // T, columns), BF16),
        in_specs=[pl.BlockSpec(memory_space=pltpu.HBM)] * 6,
        out_specs=vmem,
        scratch_shapes=[
            pltpu.VMEM((3, *query.shape), BF16), pltpu.VMEM(filters.shape, F32), pltpu.VMEM((1, width), F32), dma((3,)),
            slab, slab, slab,
            pltpu.VMEM((filters.shape[0], 2, LANES), F32), pltpu.VMEM((S, 2, LANES), F32),
            pltpu.VMEM((S + 1, 2, LANES, BLOCK), BF16),
            pltpu.VMEM((S * SLAB, UNROLL * BLOCK), BF16),
            pltpu.VMEM((S * SLAB, BLOCK), F32),
            slab, slab, slab, slab, slab,
            pltpu.VMEM((2, BLOCK, width), BF16),
            pltpu.VMEM((2, CHUNKS, width, chunk), BF16),
            pltpu.VMEM((CHUNKS, Y, rows, chunk), F32),
            pltpu.VMEM((CHUNKS, Y - 1, rows, chunk), BF16),
            pltpu.VMEM((CHUNKS, Y - 1, rows, chunk), BF16),
            pltpu.VMEM((CHUNKS, rows // 2, chunk), BF16),
            dma((1,)), dma((1,)), dma((1,)), dma((1,)), dma((1,)), dma((GROUPS_OF_SLABS,)),
            dma((1,)), dma((GROUPS_OF_SLABS,)),
            dma((1,)),
            dma((1,)), dma((CHUNKS // 2,)), dma((1,)), dma((CHUNKS // 2,)),
            dma((1,)), dma((CHUNKS, Y - 1)),
            dma((1,)), dma((1,)),
        ],
        compiler_params=pltpu.CompilerParams(
            collective_id=0, has_side_effects=True, vmem_limit_bytes=60 * 2**20
        ),
        name="hyena",
    )(query, key_branch, value, filters, skip.reshape(1, width), weight)


def solution(mesh):
    return jax.shard_map(
        body,
        mesh=mesh,
        in_specs=(
            P("seq", "tensor"),
            P("seq", "tensor"),
            P("seq", "tensor"),
            P("tensor", "seq"),
            P("tensor"),
            P("tensor", None),
        ),
        out_specs=P(("seq", "tensor"), None),
        check_vma=False,
    )
```

time: 68.9 us -> 65.5 us (0.951)
  the two profiles are of different devices: /device:TPU:2 before, /device:TPU:6 now
where the time goes in v3:
time: 65.5 us; the launch traced here: 65.3 us
  Pallas kernels  63.6 us (97%)
  local copies, waits for them, and re-layouts  1.67 us (3%)
    pallas_call x1, Pallas kernels, body(): pl.pallas_call(functools.partial(kernel, S, Y), out_shape=jax.ShapeDtypeS...  63.6 us
    unnamed x1, local copies, waits for them, and re-layouts  1.67 us

profile of v3, /device:TPU:6, one launch (start us, length us, event | category | flops | bytes accessed | tf_op | source)
XLA Modules:
  0.0 65.3 jit_solution(297694689825923187)
XLA Ops:
  0.0 63.6 %hyena.1 = bf16[16,8192]{1,0:T(8,128)(2,1)} custom-call(bf16[256,256]{1,0:T(8,128)(2,1)} %query_in.1, bf16[256,256]{1,0:T(8,128)(2,1)} %key_in.1, bf16[256,256]{1,0:T(8,128)(2,1)} %value_in.1, f32[16,256]{1,0:T(8,128)} %filters_in.1, f32[1,256]{1,0:T(1,128)} %bitcast.1, bf16[256,8192]{1,0:T(8,128)(2,1)} %weight.1), custom_call_target="tpu_custom_call" | custom-call | tf_op jit(solution)/shard_map/hyena/pallas_call | solution.py:348
  63.6 1.7 %copy.8 = bf16[16,8192]{1,0:T(8,128)(2,1)} copy(bf16[16,8192]{1,0:T(8,128)(2,1)} %hyena.1) | data formatting | bytes 524288

commit v4 on v3

--- a/solution.py
+++ b/solution.py
@@ -32,9 +32,9 @@
     S, Y,
     query_in, key_in, value_in, filters_in, skip_in, weight, out,
     factors, filters, skip, i_sem,
-    sx, rx, sq, sf, rf, toeplitz, lhs, acc, sg, rg, gk, gx, gs, gated, wv, part, ss, sr, fo,
-    x_send, x_recv, f_send, f_recv, g_send, g_recv, e_send, e_recv,
-    w_local, wd_send, wd_recv, wf_send, wf_recv, r_send, r_recv, o_send, o_recv,
+    sx, rx, sq, sf, rf, toeplitz, lhs, acc, sg, rg, gk, gx, gs, qx, hx, gated, wv, part, ss, sr, lr, fo, fr, result,
+    x_send, x_recv, f_send, f_recv, g_send, g_recv, e_send, e_recv, h_send, h_recv,
+    w_local, wd_send, wd_recv, wf_send, wf_recv, r_send, r_recv, l_recv, p_sem, o_sem,
 ):
     seq = lax.axis_index("seq")
     ten = lax.axis_index("tensor")
@@ -46,6 +46,7 @@
     beside = (seq + 1 - 2 * core, ten)
     ahead = (seq, (ten + 2) % (2 * Y))
     behind = (seq, (ten + 2 * Y - 2) % (2 * Y))
+    neighbours = ((ahead, (seq, (ten + 3 - 2 * xl) % (2 * Y))), (behind, (seq, (ten + 2 * Y - 1 - 2 * xl) % (2 * Y))))
     width = factors.shape[2]
     columns = weight.shape[1]
     wide = columns // 2
@@ -69,7 +70,7 @@
     def greet(device):
         pl.semaphore_signal(barrier, inc=1, device_id=device, device_id_type=pl.DeviceIdType.MESH)
 
-    for device in (across, around, ahead, behind):
+    for device in (across, around, *neighbours[0], *neighbours[1]):
         greet(device)
 
     def greet_seq(d, _):
@@ -77,6 +78,8 @@
         return 0
 
     lax.fori_loop(1, S, greet_seq, 0)
+    for k in range(1, group):
+        greet(((seq + k) % S, ten + 1 - 2 * xl))
 
     def own_weight(j):
         return pltpu.make_async_copy(
@@ -103,7 +106,7 @@
     rx[pl.ds(seq, 1)] = sx[pl.ds(seq, 1)]
     rf[pl.ds(seq, 1)] = sf[pl.ds(seq // 2, 1)]
 
-    pl.semaphore_wait(barrier, S + 3)
+    pl.semaphore_wait(barrier, S + 4 + group)
 
     def taps_copy(k):
         p = (seq + S - k) % S
@@ -116,6 +119,10 @@
     def response_copy(k):
         p = (seq + S - k) % S
         return remote(sg.at[p], rg.at[k], g_send.at[0], g_recv.at[k // group], (p, ten))
+
+    def twin_copy(k):
+        p = (seq + S - k) % S
+        return remote(sg.at[p], hx.at[k], h_send.at[0], h_recv.at[0], (p, ten + 1 - 2 * xl))
 
     def relay(n):
         span = pl.ds(n * group, group)
@@ -137,6 +144,8 @@
     each(lambda k: taps_copy(k).start())
     each(lambda k: signal_copy(k).start())
     sq[...] = slabs(factors[2].astype(F32))
+    for k in range(group):
+        remote(sq.at[(seq + k) % S], qx.at[k], h_send.at[1], h_recv.at[1], across).start()
 
     def direct(i):
         j = core * half + i
@@ -160,7 +169,9 @@
     all_taps = remote(rf.at[everyone], rf.at[everyone], f_send.at[0], f_recv.at[0], across)
     all_signals = remote(rx.at[everyone], rx.at[everyone], x_send.at[0], x_recv.at[0], across)
     all_responses = remote(sg.at[everyone], rg.at[everyone], g_send.at[0], g_recv.at[0], across)
-    all_relays = remote(gk, gx, e_send.at[0], e_recv.at[0], across)
+    far = pl.ds(group, S - group)
+    all_relays = remote(gk.at[far], gx.at[far], e_send.at[0], e_recv.at[0], across)
+    all_twins = remote(hx, hx, h_send.at[0], h_recv.at[0], across)
 
     def some_responses(n):
         span = pl.ds(0, group if n > 0 else group - 1)
@@ -214,11 +225,10 @@
         pieces.append(response + scale[None] * rx[...].astype(F32)[:, h * SLAB : (h + 1) * SLAB])
     sg[...] = jnp.concatenate(pieces, axis=1).astype(BF16)
     each(lambda k: response_copy(k).start())
+    for k in range(group):
+        twin_copy(k).start()
     rg[pl.ds(0, 1)] = sg[pl.ds(seq, 1)]
 
-    for i in range(half // 2):
-        direct(i).wait_recv()
-        forward(i).start()
     pltpu.make_async_copy(wv.at[0], wv.at[0], w_local.at[0]).wait()
 
     def turn(side):
@@ -233,7 +243,11 @@
             slab = (sq[s].astype(F32) * rg[k].astype(F32)).astype(BF16)
             gk[k] = slab
             gs[s] = slab
-        relay(n).start()
+        if n > 0:
+            relay(n).start()
+    for i in range(half // 2):
+        direct(i).wait_recv()
+        forward(i).start()
     turn(0)
 
     def chunk_of(i, parity):
@@ -241,17 +255,29 @@
 
     for i in range(CHUNKS):
         term = jnp.dot(gated[0], wv[0, chunk_of(i, i % 2)], preferred_element_type=F32)
-        part[i] = term.reshape(Y, rows, chunk)
+        part[i] = term.reshape(Y, 2, rows // 2, chunk)
+    remote(qx, qx, h_send.at[1], h_recv.at[1], across).wait()
+    all_twins.wait_recv()
+    for k in range(group):
+        s = (seq + k) % S
+        gs[s] = (qx[k].astype(F32) * hx[k].astype(F32)).astype(BF16)
     for n in order:
-        relay(n).wait_recv()
-    for k in range(S):
+        if n > 0:
+            relay(n).wait_recv()
+    for k in range(group, S):
         gs[(seq + k) % S] = gx[k]
     turn(1)
 
     steps = [((Y - 1) // 2, Y // 2), (Y // 2, (Y - 1) // 2)]
 
-    def hop(i, slot, device):
-        return remote(ss.at[i, slot], sr.at[i, slot], r_send.at[0], r_recv.at[i, slot], device)
+    def hop(i, slot, target, device):
+        return remote(ss.at[i, slot], sr.at[i, target], r_send.at[0], r_recv.at[i, target], device)
+
+    def last_hop(i, slot, side, apart):
+        half_rows = ss.at[i, slot, (xl + apart) % 2]
+        return remote(
+            half_rows, lr.at[i, side, apart], r_send.at[0], l_recv.at[i, side, apart], neighbours[side][apart]
+        )
 
     def pairs(batch, function):
         def step(pair, _):
@@ -264,42 +290,40 @@
     def project(i, parity):
         j = chunk_of(i, parity)
         term = jnp.dot(gated[1], wv[1, j], preferred_element_type=F32)
-        part[i] += term.reshape(Y, rows, chunk)
+        part[i] += term.reshape(Y, 2, rows // 2, chunk)
+        fo[i] = part[i, y, 1 - xl].astype(BF16)
+        remote(fo.at[i], fr.at[i], p_sem.at[0], p_sem.at[1], across).start()
         advance(0, i, parity)
 
     def advance(s, i, parity):
         up, low = steps[parity]
-        for slot, count, device, owner in (
-            (0, up, ahead, (y + up - s) % Y),
-            (up, low, behind, (y + Y - low + s) % Y),
+        for side, slot, first, count, owner in (
+            (0, 0, 0, up, (y + up - s) % Y),
+            (1, up, up - 1, low, (y + Y - low + s) % Y),
         ):
             if s >= count:
                 continue
             total = part[i, owner]
             if s > 0:
-                hop(i, slot + s - 1, device).wait_recv()
-                total = total + sr[i, slot + s - 1].astype(F32)
+                hop(i, slot + s - 1, first + s - 1, neighbours[side][0]).wait_recv()
+                total = total + sr[i, first + s - 1].astype(F32)
             ss[i, slot + s] = total.astype(BF16)
-            hop(i, slot + s, device).start()
-
-    def deliver(i, parity):
+            if s < count - 1:
+                hop(i, slot + s, first + s, neighbours[side][0]).start()
+            else:
+                last_hop(i, slot + s, side, 0).start()
+                last_hop(i, slot + s, side, 1).start()
+
+    def finish(i, parity):
         j = chunk_of(i, parity)
-        place = pl.ds(pl.multiple_of(xl * wide + j * chunk, LANES), chunk)
-        return remote(fo.at[i], out.at[:, place], o_send.at[0], o_recv.at[0], across)
-
-    def finish(i, parity):
-        up, low = steps[parity]
-        j = chunk_of(i, parity)
-        total = part[i, y]
-        for slot, count, device in ((0, up, ahead), (up, low, behind)):
-            if count:
-                hop(i, slot + count - 1, device).wait_recv()
-                total = total + sr[i, slot + count - 1].astype(F32)
-        mine = jnp.where(xl == 0, total[: rows // 2], total[rows // 2 :])
-        other = jnp.where(xl == 0, total[rows // 2 :], total[: rows // 2])
-        fo[i] = other.astype(BF16)
-        deliver(i, parity).start()
-        out[:, pl.ds(pl.multiple_of(xl * wide + j * chunk, LANES), chunk)] = mine.astype(BF16)
+        for apart in range(2):
+            total = part[i, y, xl] if apart == 0 else fr[i].astype(F32)
+            for side in range(2):
+                last_hop(i, 0, side, apart).wait_recv()
+                total = total + lr[i, side, apart].astype(F32)
+            place = pl.ds(pl.multiple_of((xl + apart) % 2 * wide + j * chunk, LANES), chunk)
+            result[:, place] = total.astype(BF16)
+            pltpu.make_async_copy(result.at[:, place], out.at[:, place], o_sem.at[0]).start()
 
     for i in range(half):
         if i % 2 == 1:
@@ -309,6 +333,7 @@
     all_signals.wait_send()
     all_responses.wait_send()
     all_relays.wait_send()
+    all_twins.wait_send()
     for n in range(half // 2, half):
         direct(n).wait_recv()
         forward(n).start()
@@ -320,6 +345,7 @@
     for s in range(2, Y // 2):
         pairs(0, functools.partial(advance, s))
         pairs(1, functools.partial(advance, s - 1))
+    remote(fo, fr, p_sem.at[0], p_sem.at[1], across).wait()
     pairs(0, finish)
     if Y // 2 > 1:
         pairs(1, functools.partial(advance, Y // 2 - 1))
@@ -327,11 +353,8 @@
 
     remote(wv.at[0, pl.ds(0, half)], wv.at[0, pl.ds(0, half)], wd_send.at[0], wd_recv.at[0], across).wait_send()
     remote(wv.at[1, pl.ds(0, half)], wv.at[1, pl.ds(0, half)], wf_send.at[0], wf_recv.at[0], beside).wait_send()
-    remote(ss, sr, r_send.at[0], r_recv.at[0, 0], ahead).wait_send()
-    other = out.at[:, pl.ds(pl.multiple_of((1 - xl) * wide, LANES), wide)]
-    delivered = remote(other, other, o_send.at[0], o_recv.at[0], across)
-    delivered.wait_send()
-    delivered.wait_recv()
+    remote(ss, ss, r_send.at[0], p_sem.at[1], ahead).wait_send()
+    pltpu.make_async_copy(result, out, o_sem.at[0]).wait()
 
 
 def body(query, key_branch, value, filters, skip, weight):
@@ -342,14 +365,13 @@
     columns = weight.shape[1]
     chunk = columns // 2 // CHUNKS
     rows = BLOCK // Y
-    vmem = pl.BlockSpec(memory_space=pltpu.VMEM)
     dma = pltpu.SemaphoreType.DMA
     slab = pltpu.VMEM((S, 2 * SLAB, LANES), BF16)
     return pl.pallas_call(
         functools.partial(kernel, S, Y),
         out_shape=jax.ShapeDtypeStruct((BLOCK // T, columns), BF16),
         in_specs=[pl.BlockSpec(memory_space=pltpu.HBM)] * 6,
-        out_specs=vmem,
+        out_specs=pl.BlockSpec(memory_space=pltpu.HBM),
         scratch_shapes=[
             pltpu.VMEM((3, *query.shape), BF16), pltpu.VMEM(filters.shape, F32), pltpu.VMEM((1, width), F32), dma((3,)),
             slab, slab, slab,
@@ -358,18 +380,21 @@
             pltpu.VMEM((S * SLAB, UNROLL * BLOCK), BF16),
             pltpu.VMEM((S * SLAB, BLOCK), F32),
             slab, slab, slab, slab, slab,
+            pltpu.VMEM((S // GROUPS_OF_SLABS, 2 * SLAB, LANES), BF16), pltpu.VMEM((S // GROUPS_OF_SLABS, 2 * SLAB, LANES), BF16),
             pltpu.VMEM((2, BLOCK, width), BF16),
             pltpu.VMEM((2, CHUNKS, width, chunk), BF16),
-            pltpu.VMEM((CHUNKS, Y, rows, chunk), F32),
-            pltpu.VMEM((CHUNKS, Y - 1, rows, chunk), BF16),
-            pltpu.VMEM((CHUNKS, Y - 1, rows, chunk), BF16),
+            pltpu.VMEM((CHUNKS, Y, 2, rows // 2, chunk), F32),
+            pltpu.VMEM((CHUNKS, Y - 1, 2, rows // 2, chunk), BF16),
+            pltpu.VMEM((CHUNKS, Y - 3, 2, rows // 2, chunk), BF16),
+            pltpu.VMEM((CHUNKS, 2, 2, rows // 2, chunk), BF16),
             pltpu.VMEM((CHUNKS, rows // 2, chunk), BF16),
+            pltpu.VMEM((CHUNKS, rows // 2, chunk), BF16),
+            pltpu.VMEM((BLOCK // T, columns), BF16),
             dma((1,)), dma((1,)), dma((1,)), dma((1,)), dma((1,)), dma((GROUPS_OF_SLABS,)),
-            dma((1,)), dma((GROUPS_OF_SLABS,)),
+            dma((1,)), dma((GROUPS_OF_SLABS,)), dma((2,)), dma((2,)),
             dma((1,)),
             dma((1,)), dma((CHUNKS // 2,)), dma((1,)), dma((CHUNKS // 2,)),
-            dma((1,)), dma((CHUNKS, Y - 1)),
-            dma((1,)), dma((1,)),
+            dma((1,)), dma((CHUNKS, Y - 3)), dma((CHUNKS, 2, 2)), dma((2,)), dma((1,)),
         ],
         compiler_params=pltpu.CompilerParams(
             collective_id=0, has_side_effects=True, vmem_limit_bytes=60 * 2**20

time: 65.5 us -> 63.8 us (0.974)
  Pallas kernels: 63.6 us -> 61.9 us
    pallas_call x1, Pallas kernels: 63.6 us -> 61.9 us  [body(): pl.pallas_call(functools.partial(kernel, S, Y), out_shape=jax.ShapeDtypeS...]
where the time goes in v4:
time: 63.8 us; the launch traced here: 63.6 us
  Pallas kernels  61.9 us (97%)
  local copies, waits for them, and re-layouts  1.67 us (3%)
    pallas_call x1, Pallas kernels, body(): pl.pallas_call(functools.partial(kernel, S, Y), out_shape=jax.ShapeDtypeS...  61.9 us
    unnamed x1, local copies, waits for them, and re-layouts  1.67 us

profile of v4, /device:TPU:6, one launch (start us, length us, event | category | flops | bytes accessed | tf_op | source)
XLA Modules:
  0.0 63.6 jit_solution(4139554271935270388)
XLA Ops:
  0.0 61.9 %hyena.1 = bf16[16,8192]{1,0:T(8,128)(2,1)} custom-call(bf16[256,256]{1,0:T(8,128)(2,1)} %query_in.1, bf16[256,256]{1,0:T(8,128)(2,1)} %key_in.1, bf16[256,256]{1,0:T(8,128)(2,1)} %value_in.1, f32[16,256]{1,0:T(8,128)} %filters_in.1, f32[1,256]{1,0:T(1,128)} %bitcast.1, bf16[256,8192]{1,0:T(8,128)(2,1)} %weight.1), custom_call_target="tpu_custom_call" | custom-call | tf_op jit(solution)/shard_map/hyena/pallas_call | solution.py:370
  61.9 1.7 %copy.8 = bf16[16,8192]{1,0:T(8,128)(2,1)} copy(bf16[16,8192]{1,0:T(8,128)(2,1)} %hyena.1) | data formatting | bytes 524288

commit v5 on v4

--- a/solution.py
+++ b/solution.py
@@ -32,9 +32,9 @@
     S, Y,
     query_in, key_in, value_in, filters_in, skip_in, weight, out,
     factors, filters, skip, i_sem,
-    sx, rx, sq, sf, rf, toeplitz, lhs, acc, sg, rg, gk, gx, gs, qx, hx, gated, wv, part, ss, sr, lr, fo, fr, result,
+    sx, rx, sq, sf, rf, toeplitz, lhs, acc, sg, rg, gk, gx, gs, qx, hx, gated, wv, part, ss, sr, lr, fo, fr,
     x_send, x_recv, f_send, f_recv, g_send, g_recv, e_send, e_recv, h_send, h_recv,
-    w_local, wd_send, wd_recv, wf_send, wf_recv, r_send, r_recv, l_recv, p_sem, o_sem,
+    w_local, wd_send, wd_recv, wf_send, wf_recv, r_send, r_recv, l_recv, p_sem,
 ):
     seq = lax.axis_index("seq")
     ten = lax.axis_index("tensor")
@@ -77,7 +77,7 @@
         greet(((seq + d) % S, ten))
         return 0
 
-    lax.fori_loop(1, S, greet_seq, 0)
+    lax.fori_loop(1, S, greet_seq, 0, unroll=True)
     for k in range(1, group):
         greet(((seq + k) % S, ten + 1 - 2 * xl))
 
@@ -270,13 +270,15 @@
 
     steps = [((Y - 1) // 2, Y // 2), (Y // 2, (Y - 1) // 2)]
 
-    def hop(i, slot, target, device):
-        return remote(ss.at[i, slot], sr.at[i, target], r_send.at[0], r_recv.at[i, target], device)
+    def hop(i, slot, s, side):
+        return remote(
+            ss.at[i, slot], sr.at[i, s, side], r_send.at[0], r_recv.at[i, s], neighbours[side][0]
+        )
 
     def last_hop(i, slot, side, apart):
         half_rows = ss.at[i, slot, (xl + apart) % 2]
         return remote(
-            half_rows, lr.at[i, side, apart], r_send.at[0], l_recv.at[i, side, apart], neighbours[side][apart]
+            half_rows, lr.at[i, side, apart], r_send.at[0], l_recv.at[i], neighbours[side][apart]
         )
 
     def pairs(batch, function):
@@ -297,33 +299,32 @@
 
     def advance(s, i, parity):
         up, low = steps[parity]
-        for side, slot, first, count, owner in (
-            (0, 0, 0, up, (y + up - s) % Y),
-            (1, up, up - 1, low, (y + Y - low + s) % Y),
-        ):
+        if 0 < s < min(up, low):
+            remote(sr.at[i, s - 1], sr.at[i, s - 1], r_send.at[0], r_recv.at[i, s - 1], ahead).wait_recv()
+        elif 0 < s < max(up, low):
+            hop(i, 0, s - 1, 0 if up > low else 1).wait_recv()
+        for side, slot, count, owner in ((0, 0, up, (y + up - s) % Y), (1, up, low, (y + Y - low + s) % Y)):
             if s >= count:
                 continue
             total = part[i, owner]
             if s > 0:
-                hop(i, slot + s - 1, first + s - 1, neighbours[side][0]).wait_recv()
-                total = total + sr[i, first + s - 1].astype(F32)
+                total = total + sr[i, s - 1, side].astype(F32)
             ss[i, slot + s] = total.astype(BF16)
             if s < count - 1:
-                hop(i, slot + s, first + s, neighbours[side][0]).start()
+                hop(i, slot + s, s, side).start()
             else:
                 last_hop(i, slot + s, side, 0).start()
                 last_hop(i, slot + s, side, 1).start()
 
     def finish(i, parity):
         j = chunk_of(i, parity)
+        remote(lr.at[i], lr.at[i], r_send.at[0], l_recv.at[i], ahead).wait_recv()
         for apart in range(2):
             total = part[i, y, xl] if apart == 0 else fr[i].astype(F32)
             for side in range(2):
-                last_hop(i, 0, side, apart).wait_recv()
                 total = total + lr[i, side, apart].astype(F32)
             place = pl.ds(pl.multiple_of((xl + apart) % 2 * wide + j * chunk, LANES), chunk)
-            result[:, place] = total.astype(BF16)
-            pltpu.make_async_copy(result.at[:, place], out.at[:, place], o_sem.at[0]).start()
+            out[:, place] = total.astype(BF16)
 
     for i in range(half):
         if i % 2 == 1:
@@ -337,24 +338,25 @@
     for n in range(half // 2, half):
         direct(n).wait_recv()
         forward(n).start()
+    last = Y // 2 - 1
     pairs(0, functools.partial(advance, 1))
     for i in range(half, CHUNKS):
         if i % 2 == 1:
             forwarded(i // 2).wait_recv()
         project(i, i % 2)
-    for s in range(2, Y // 2):
+    for s in range(2, last):
         pairs(0, functools.partial(advance, s))
-        pairs(1, functools.partial(advance, s - 1))
+    for s in range(1, last):
+        pairs(1, functools.partial(advance, s))
+    pairs(0, functools.partial(advance, last))
     remote(fo, fr, p_sem.at[0], p_sem.at[1], across).wait()
+    pairs(1, functools.partial(advance, last))
     pairs(0, finish)
-    if Y // 2 > 1:
-        pairs(1, functools.partial(advance, Y // 2 - 1))
     pairs(1, finish)
 
     remote(wv.at[0, pl.ds(0, half)], wv.at[0, pl.ds(0, half)], wd_send.at[0], wd_recv.at[0], across).wait_send()
     remote(wv.at[1, pl.ds(0, half)], wv.at[1, pl.ds(0, half)], wf_send.at[0], wf_recv.at[0], beside).wait_send()
     remote(ss, ss, r_send.at[0], p_sem.at[1], ahead).wait_send()
-    pltpu.make_async_copy(result, out, o_sem.at[0]).wait()
 
 
 def body(query, key_branch, value, filters, skip, weight):
@@ -369,9 +371,9 @@
     slab = pltpu.VMEM((S, 2 * SLAB, LANES), BF16)
     return pl.pallas_call(
         functools.partial(kernel, S, Y),
-        out_shape=jax.ShapeDtypeStruct((BLOCK // T, columns), BF16),
+        out_shape=pltpu.VMEM((BLOCK // T, columns), BF16),
         in_specs=[pl.BlockSpec(memory_space=pltpu.HBM)] * 6,
-        out_specs=pl.BlockSpec(memory_space=pltpu.HBM),
+        out_specs=pl.BlockSpec(memory_space=pltpu.VMEM),
         scratch_shapes=[
             pltpu.VMEM((3, *query.shape), BF16), pltpu.VMEM(filters.shape, F32), pltpu.VMEM((1, width), F32), dma((3,)),
             slab, slab, slab,
@@ -385,16 +387,15 @@
             pltpu.VMEM((2, CHUNKS, width, chunk), BF16),
             pltpu.VMEM((CHUNKS, Y, 2, rows // 2, chunk), F32),
             pltpu.VMEM((CHUNKS, Y - 1, 2, rows // 2, chunk), BF16),
-            pltpu.VMEM((CHUNKS, Y - 3, 2, rows // 2, chunk), BF16),
+            pltpu.VMEM((CHUNKS, Y // 2 - 1, 2, 2, rows // 2, chunk), BF16),
             pltpu.VMEM((CHUNKS, 2, 2, rows // 2, chunk), BF16),
             pltpu.VMEM((CHUNKS, rows // 2, chunk), BF16),
             pltpu.VMEM((CHUNKS, rows // 2, chunk), BF16),
-            pltpu.VMEM((BLOCK // T, columns), BF16),
             dma((1,)), dma((1,)), dma((1,)), dma((1,)), dma((1,)), dma((GROUPS_OF_SLABS,)),
             dma((1,)), dma((GROUPS_OF_SLABS,)), dma((2,)), dma((2,)),
             dma((1,)),
             dma((1,)), dma((CHUNKS // 2,)), dma((1,)), dma((CHUNKS // 2,)),
-            dma((1,)), dma((CHUNKS, Y - 3)), dma((CHUNKS, 2, 2)), dma((2,)), dma((1,)),
+            dma((1,)), dma((CHUNKS, Y // 2 - 1)), dma((CHUNKS,)), dma((2,)),
         ],
         compiler_params=pltpu.CompilerParams(
             collective_id=0, has_side_effects=True, vmem_limit_bytes=60 * 2**20

time: 63.8 us -> 60.7 us (0.951)
  Pallas kernels: 61.9 us -> 59.9 us
  local copies, waits for them, and re-layouts: 1.67 us -> 0.71 us
    pallas_call x1, Pallas kernels: 61.9 us -> 59.9 us  [body(): pl.pallas_call(functools.partial(kernel, S, Y), out_shape=pltpu.VMEM((BLO...]
    unnamed x1, local copies, waits for them, and re-layouts: 1.67 us -> 0.71 us
where the time goes in v5:
time: 60.7 us; the launch traced here: 60.6 us
  Pallas kernels  59.9 us (99%)
  local copies, waits for them, and re-layouts  0.71 us (1%)
    pallas_call x1, Pallas kernels, body(): pl.pallas_call(functools.partial(kernel, S, Y), out_shape=pltpu.VMEM((BLO...  59.9 us

profile of v5, /device:TPU:6, one launch (start us, length us, event | category | flops | bytes accessed | tf_op | source)
XLA Modules:
  0.0 60.6 jit_solution(16883308556950786181)
XLA Ops:
  0.0 59.9 %hyena.1 = bf16[16,8192]{1,0:T(8,128)(2,1)S(1)} custom-call(bf16[256,256]{1,0:T(8,128)(2,1)} %query_in.1, bf16[256,256]{1,0:T(8,128)(2,1)} %key_in.1, bf16[256,256]{1,0:T(8,128)(2,1)} %value_in.1, f32[16,256]{1,0:T(8,128)} %filters_in.1, f32[1,256]{1,0:T(1,128)} %bitcast.1, bf16[256,8192]{1,0:T(8,128)(2,1)} %weight.1), custom_call_target="tpu_custom_call" | custom-call | tf_op jit(solution)/shard_map/hyena/pallas_call | solution.py:372
  59.9 0.7 %copy.8 = bf16[16,8192]{1,0:T(8,128)(2,1)} copy(bf16[16,8192]{1,0:T(8,128)(2,1)S(1)} %hyena.1) | data formatting | bytes 524288

commit v6 on v5

--- a/solution.py
+++ b/solution.py
@@ -130,16 +130,15 @@
 
     order = [GROUPS_OF_SLABS // 2, GROUPS_OF_SLABS // 2 - 1] + list(range(GROUPS_OF_SLABS // 2 + 1, GROUPS_OF_SLABS)) + [0]
 
-    def each_of(n, function):
-        def step(k, _):
-            function(k)
+    def each(function):
+        function(S // 2)
+
+        def step(m, _):
+            function(S // 2 - m)
+            function(S // 2 + m)
             return 0
 
-        lax.fori_loop(max(n * group, 1), (n + 1) * group, step, 0)
-
-    def each(function):
-        for n in order:
-            each_of(n, function)
+        lax.fori_loop(1, S // 2, step, 0, unroll=True)
 
     each(lambda k: taps_copy(k).start())
     each(lambda k: signal_copy(k).start())

time: 60.7 us -> 60.4 us (level)
  no operation moved by 1% of the time
where the time goes in v6:
time: 60.4 us; the launch traced here: 60.3 us
  Pallas kernels  59.6 us (99%)
  local copies, waits for them, and re-layouts  0.71 us (1%)
    pallas_call x1, Pallas kernels, body(): pl.pallas_call(functools.partial(kernel, S, Y), out_shape=pltpu.VMEM((BLO...  59.6 us

profile of v6, /device:TPU:6, one launch (start us, length us, event | category | flops | bytes accessed | tf_op | source)
XLA Modules:
  0.0 60.3 jit_solution(18428756331922117222)
XLA Ops:
  0.0 59.6 %hyena.1 = bf16[16,8192]{1,0:T(8,128)(2,1)S(1)} custom-call(bf16[256,256]{1,0:T(8,128)(2,1)} %query_in.1, bf16[256,256]{1,0:T(8,128)(2,1)} %key_in.1, bf16[256,256]{1,0:T(8,128)(2,1)} %value_in.1, f32[16,256]{1,0:T(8,128)} %filters_in.1, f32[1,256]{1,0:T(1,128)} %bitcast.1, bf16[256,8192]{1,0:T(8,128)(2,1)} %weight.1), custom_call_target="tpu_custom_call" | custom-call | tf_op jit(solution)/shard_map/hyena/pallas_call | solution.py:371
  59.6 0.7 %copy.8 = bf16[16,8192]{1,0:T(8,128)(2,1)} copy(bf16[16,8192]{1,0:T(8,128)(2,1)S(1)} %hyena.1) | data formatting | bytes 524288

commit v7 on v6

--- a/solution.py
+++ b/solution.py
@@ -10,7 +10,7 @@
 F32 = jnp.float32
 BF16 = jnp.bfloat16
 LANES = 128
-GROUPS_OF_SLABS = 4
+GROUPS_OF_SLABS = 8
 SLAB = 8
 BLOCK = 2 * LANES
 UNROLL = 4
@@ -54,6 +54,7 @@
     half = CHUNKS // 2
     rows = BLOCK // Y
     group = S // GROUPS_OF_SLABS
+    near = range(-group, 2 * group)
 
     inputs = [
         pltpu.make_async_copy(key_in, factors.at[0], i_sem.at[0]),
@@ -78,8 +79,9 @@
         return 0
 
     lax.fori_loop(1, S, greet_seq, 0, unroll=True)
-    for k in range(1, group):
-        greet(((seq + k) % S, ten + 1 - 2 * xl))
+    for k in near:
+        if k != 0:
+            greet(((seq + S + k) % S, ten + 1 - 2 * xl))
 
     def own_weight(j):
         return pltpu.make_async_copy(
@@ -106,7 +108,7 @@
     rx[pl.ds(seq, 1)] = sx[pl.ds(seq, 1)]
     rf[pl.ds(seq, 1)] = sf[pl.ds(seq // 2, 1)]
 
-    pl.semaphore_wait(barrier, S + 4 + group)
+    pl.semaphore_wait(barrier, S + 4 + 3 * group)
 
     def taps_copy(k):
         p = (seq + S - k) % S
@@ -122,13 +124,18 @@
 
     def twin_copy(k):
         p = (seq + S - k) % S
-        return remote(sg.at[p], hx.at[k], h_send.at[0], h_recv.at[0], (p, ten + 1 - 2 * xl))
+        return remote(sg.at[p], hx.at[k + group], h_send.at[0], h_recv.at[0], (p, ten + 1 - 2 * xl))
 
     def relay(n):
         span = pl.ds(n * group, group)
         return remote(gk.at[span], gx.at[span], e_send.at[0], e_recv.at[n], across)
 
-    order = [GROUPS_OF_SLABS // 2, GROUPS_OF_SLABS // 2 - 1] + list(range(GROUPS_OF_SLABS // 2 + 1, GROUPS_OF_SLABS)) + [0]
+    middle = GROUPS_OF_SLABS // 2
+    order = [middle]
+    for n in range(1, middle):
+        order += [middle - n, middle + n]
+    order += [0]
+    far = order[:-3]
 
     def each(function):
         function(S // 2)
@@ -143,8 +150,8 @@
     each(lambda k: taps_copy(k).start())
     each(lambda k: signal_copy(k).start())
     sq[...] = slabs(factors[2].astype(F32))
-    for k in range(group):
-        remote(sq.at[(seq + k) % S], qx.at[k], h_send.at[1], h_recv.at[1], across).start()
+    for k in near:
+        remote(sq.at[(seq + S + k) % S], qx.at[k + group], h_send.at[1], h_recv.at[1], across).start()
 
     def direct(i):
         j = core * half + i
@@ -161,15 +168,25 @@
         j = (1 - core) * half + i
         return remote(wv.at[1, j], wv.at[1, j], wf_send.at[0], wf_recv.at[i], beside)
 
-    for i in range(half):
+    def direct_part(i, part_of):
+        j = core * half + i
+        span = pl.ds(part_of * (width // 2), width // 2)
+        place = pl.ds(pl.multiple_of((1 - xl) * wide + j * chunk, LANES), chunk)
+        return remote(
+            weight.at[span, place], wv.at[1, j, span], wd_send.at[0], wd_recv.at[i], across if i % 2 == 0 else around
+        )
+
+    for i in range(half // 2):
         direct(i).start()
+    for i in range(half // 2, half):
+        direct_part(i, 0).start()
 
     everyone = pl.ds(0, S - 1)
     all_taps = remote(rf.at[everyone], rf.at[everyone], f_send.at[0], f_recv.at[0], across)
     all_signals = remote(rx.at[everyone], rx.at[everyone], x_send.at[0], x_recv.at[0], across)
     all_responses = remote(sg.at[everyone], rg.at[everyone], g_send.at[0], g_recv.at[0], across)
-    far = pl.ds(group, S - group)
-    all_relays = remote(gk.at[far], gx.at[far], e_send.at[0], e_recv.at[0], across)
+    relayed = pl.ds(2 * group, S - 3 * group)
+    all_relays = remote(gk.at[relayed], gx.at[relayed], e_send.at[0], e_recv.at[0], across)
     all_twins = remote(hx, hx, h_send.at[0], h_recv.at[0], across)
 
     def some_responses(n):
@@ -224,8 +241,10 @@
         pieces.append(response + scale[None] * rx[...].astype(F32)[:, h * SLAB : (h + 1) * SLAB])
     sg[...] = jnp.concatenate(pieces, axis=1).astype(BF16)
     each(lambda k: response_copy(k).start())
-    for k in range(group):
+    for k in reversed(near):
         twin_copy(k).start()
+    for i in range(half // 2, half):
+        direct_part(i, 1).start()
     rg[pl.ds(0, 1)] = sg[pl.ds(seq, 1)]
 
     pltpu.make_async_copy(wv.at[0], wv.at[0], w_local.at[0]).wait()
@@ -242,7 +261,7 @@
             slab = (sq[s].astype(F32) * rg[k].astype(F32)).astype(BF16)
             gk[k] = slab
             gs[s] = slab
-        if n > 0:
+        if n in far:
             relay(n).start()
     for i in range(half // 2):
         direct(i).wait_recv()
@@ -257,13 +276,11 @@
         part[i] = term.reshape(Y, 2, rows // 2, chunk)
     remote(qx, qx, h_send.at[1], h_recv.at[1], across).wait()
     all_twins.wait_recv()
-    for k in range(group):
-        s = (seq + k) % S
-        gs[s] = (qx[k].astype(F32) * hx[k].astype(F32)).astype(BF16)
-    for n in order:
-        if n > 0:
-            relay(n).wait_recv()
-    for k in range(group, S):
+    for k in near:
+        gs[(seq + S + k) % S] = (qx[k + group].astype(F32) * hx[k + group].astype(F32)).astype(BF16)
+    for n in far:
+        relay(n).wait_recv()
+    for k in range(2 * group, S - group):
         gs[(seq + k) % S] = gx[k]
     turn(1)
 
@@ -381,7 +398,8 @@
             pltpu.VMEM((S * SLAB, UNROLL * BLOCK), BF16),
             pltpu.VMEM((S * SLAB, BLOCK), F32),
             slab, slab, slab, slab, slab,
-            pltpu.VMEM((S // GROUPS_OF_SLABS, 2 * SLAB, LANES), BF16), pltpu.VMEM((S // GROUPS_OF_SLABS, 2 * SLAB, LANES), BF16),
+            pltpu.VMEM((3 * S // GROUPS_OF_SLABS, 2 * SLAB, LANES), BF16),
+            pltpu.VMEM((3 * S // GROUPS_OF_SLABS, 2 * SLAB, LANES), BF16),
             pltpu.VMEM((2, BLOCK, width), BF16),
             pltpu.VMEM((2, CHUNKS, width, chunk), BF16),
             pltpu.VMEM((CHUNKS, Y, 2, rows // 2, chunk), F32),

time: 60.4 us -> 60.1 us (level); the launches traced: 60.3 us -> 59.3 us
  Pallas kernels: 59.6 us -> 58.6 us
    pallas_call x1, Pallas kernels: 59.6 us -> 58.6 us  [body(): pl.pallas_call(functools.partial(kernel, S, Y), out_shape=pltpu.VMEM((BLO...]
where the time goes in v7:
time: 60.1 us; the launch traced here: 59.3 us
  Pallas kernels  58.6 us (98%)
  local copies, waits for them, and re-layouts  0.71 us (1%)
    pallas_call x1, Pallas kernels, body(): pl.pallas_call(functools.partial(kernel, S, Y), out_shape=pltpu.VMEM((BLO...  58.6 us

profile of v7, /device:TPU:6, one launch (start us, length us, event | category | flops | bytes accessed | tf_op | source)
XLA Modules:
  0.0 59.3 jit_solution(3566476540654134263)
XLA Ops:
  0.0 58.6 %hyena.1 = bf16[16,8192]{1,0:T(8,128)(2,1)S(1)} custom-call(bf16[256,256]{1,0:T(8,128)(2,1)} %query_in.1, bf16[256,256]{1,0:T(8,128)(2,1)} %key_in.1, bf16[256,256]{1,0:T(8,128)(2,1)} %value_in.1, f32[16,256]{1,0:T(8,128)} %filters_in.1, f32[1,256]{1,0:T(1,128)} %bitcast.1, bf16[256,8192]{1,0:T(8,128)(2,1)} %weight.1), custom_call_target="tpu_custom_call" | custom-call | tf_op jit(solution)/shard_map/hyena/pallas_call | solution.py:388
  58.6 0.7 %copy.8 = bf16[16,8192]{1,0:T(8,128)(2,1)} copy(bf16[16,8192]{1,0:T(8,128)(2,1)S(1)} %hyena.1) | data formatting | bytes 524288

commit v8 on v7

--- a/solution.py
+++ b/solution.py
@@ -360,10 +360,10 @@
         if i % 2 == 1:
             forwarded(i // 2).wait_recv()
         project(i, i % 2)
-    for s in range(2, last):
-        pairs(0, functools.partial(advance, s))
     for s in range(1, last):
         pairs(1, functools.partial(advance, s))
+        if s + 1 < last:
+            pairs(0, functools.partial(advance, s + 1))
     pairs(0, functools.partial(advance, last))
     remote(fo, fr, p_sem.at[0], p_sem.at[1], across).wait()
     pairs(1, functools.partial(advance, last))

time: 60.1 us -> 59.8 us (level)
  no operation moved by 1% of the time
where the time goes in v8:
time: 59.8 us; the launch traced here: 59.3 us
  Pallas kernels  58.6 us (98%)
  local copies, waits for them, and re-layouts  0.71 us (1%)
    pallas_call x1, Pallas kernels, body(): pl.pallas_call(functools.partial(kernel, S, Y), out_shape=pltpu.VMEM((BLO...  58.6 us

profile of v8, /device:TPU:6, one launch (start us, length us, event | category | flops | bytes accessed | tf_op | source)
XLA Modules:
  0.0 59.3 jit_solution(5340837161965301459)
XLA Ops:
  0.0 58.6 %hyena.1 = bf16[16,8192]{1,0:T(8,128)(2,1)S(1)} custom-call(bf16[256,256]{1,0:T(8,128)(2,1)} %query_in.1, bf16[256,256]{1,0:T(8,128)(2,1)} %key_in.1, bf16[256,256]{1,0:T(8,128)(2,1)} %value_in.1, f32[16,256]{1,0:T(8,128)} %filters_in.1, f32[1,256]{1,0:T(1,128)} %bitcast.1, bf16[256,8192]{1,0:T(8,128)(2,1)} %weight.1), custom_call_target="tpu_custom_call" | custom-call | tf_op jit(solution)/shard_map/hyena/pallas_call | solution.py:388
  58.6 0.7 %copy.8 = bf16[16,8192]{1,0:T(8,128)(2,1)} copy(bf16[16,8192]{1,0:T(8,128)(2,1)S(1)} %hyena.1) | data formatting | bytes 524288
